TPU v7x, 128 devices: a whole 4x4x4 slice. The times are simulated.
128 devices in a mesh: row: 32 (over z, y, core), col: 4 (over x).
Axes of the slice: x: 4, y: 4, z: 4, core: 2. Of those that a mesh axis runs over, the one named last changes fastest.
Arguments:
- trailing: float32 [16384, 16384], P('row', 'col'), may hold values from -40 to 40, as said below
Outputs:
- reduced: float32 [16384, 16384], P('row', 'col')
- reflectors: float32 [16384, 64], P('row')
Inputs may be any that keep to these rules, and one draw needn't show every extreme that they name: symmetric: trailing equals its transpose.
All inputs are finite; a program needn't handle non-finite values.
Results may differ from a plain program's by a relative error of at most 0.0003.
Values sent between devices are 32-bit elements; how exact they have to be, the bound alone decides.
A program may use at most 128 MiB of HBM per device.

v0:
```python
import jax
import jax.numpy as jnp
from jax import lax
from jax.sharding import PartitionSpec as P

NB = 64


highest = lax.Precision.HIGHEST


def from_root(array, axis, root):
    mine = lax.axis_index(axis) == root
    return lax.psum(jnp.where(mine, array, jnp.zeros_like(array)), axis)


def reflect_column(step_col, col_dots, pivot_row, panel_cols, row_ids):
    width = panel_cols.shape[1]
    norm_sq = col_dots[step_col]
    leading = pivot_row[step_col]
    length = jnp.sqrt(norm_sq)
    reflected = jnp.where(leading >= 0.0, -length, length)
    factor = (reflected - leading) / reflected
    scaling = 1.0 / (leading - reflected)
    active = row_ids >= NB + step_col
    on_pivot = row_ids == NB + step_col
    current = lax.dynamic_slice_in_dim(panel_cols, step_col, 1, 1)[:, 0]
    masked_col = jnp.where(active, current, 0.0)
    vector = jnp.where(on_pivot, 1.0, masked_col * scaling)
    products = (col_dots - reflected * pivot_row) * scaling
    columns = jnp.arange(width)
    later = jnp.where(columns > step_col, products, 0.0)
    panel_cols = panel_cols - factor * vector[:, None] * later[None, :]
    new_column = jnp.where(active, jnp.where(on_pivot, reflected, 0.0), current)
    panel_cols = jnp.where((columns == step_col)[None, :], new_column[:, None], panel_cols)
    return (panel_cols, vector, factor)


def block_factor(gram_refl, factors):
    width = gram_refl.shape[0]
    columns = jnp.arange(width)

    def block_turn(step_col, block):
        factor = factors[step_col]
        prior = lax.dynamic_slice_in_dim(gram_refl, step_col, 1, 1)[:, 0]
        prior = jnp.where(columns < step_col, prior, 0.0)
        column = -factor * jnp.dot(block, prior, precision=highest)
        column = jnp.where(columns == step_col, factor, column)
        return jnp.where((columns == step_col)[None, :], column[:, None], block)

    return lax.fori_loop(0, width, block_turn, jnp.zeros((width, width), jnp.float32))


def local(trailing):
    local_rows, local_cols = trailing.shape
    row_index = lax.axis_index("row")
    col_index = lax.axis_index("col")
    row_ids = row_index * local_rows + jnp.arange(local_rows)
    columns = jnp.arange(NB)
    start = (
        trailing[:, :NB],
        jnp.zeros((local_rows, NB), jnp.float32),
        jnp.zeros((NB,), jnp.float32),
    )
    first_cols = start[0]
    below = jnp.where(row_ids >= NB, 1.0, 0.0)
    local_gram = jnp.dot((first_cols * below[:, None]).T, first_cols, precision=highest)
    selector = jnp.where(row_ids[:, None] == NB + columns[None, :], 1.0, 0.0)
    local_top = jnp.dot(selector.T, first_cols, precision=highest)
    panel_gram, top_rows = lax.psum((local_gram, local_top), "row")
    top_ids = NB + columns

    def body_turn(step_col, carry):
        panel_cols, vectors, factors, top_block = carry
        finished = lax.dynamic_slice_in_dim(top_block, step_col, 1, 1)[:, 0]
        finished = jnp.where(columns < step_col, finished, 0.0)
        gram_col = lax.dynamic_slice_in_dim(panel_gram, step_col, 1, 1)[:, 0]
        col_dots = gram_col - jnp.dot(finished, top_block, precision=highest)
        pivot_row = lax.dynamic_slice_in_dim(top_block, step_col, 1, 0)[0]
        panel_cols, vector, factor = reflect_column(
            step_col, col_dots, pivot_row, panel_cols, row_ids
        )
        top_block, unused_vec, unused_fac = reflect_column(
            step_col, col_dots, pivot_row, top_block, top_ids
        )
        vectors = jnp.where((columns == step_col)[None, :], vector[:, None], vectors)
        factors = jnp.where(columns == step_col, factor, factors)
        return (panel_cols, vectors, factors, top_block)

    panel_cols, vectors, factors, top_block = lax.fori_loop(0, NB, body_turn, start + (top_rows,))
    vectors, factors = (from_root(vectors, "col", 0), from_root(factors, "col", 0))
    every_row = lax.all_gather(vectors, "row", axis=0, tiled=True)
    gram_refl = jnp.dot(every_row.T, every_row, precision=highest)
    own_cols = lax.dynamic_slice_in_dim(every_row, col_index * local_cols, local_cols, 0)
    block = block_factor(gram_refl, factors)
    row_product = lax.psum(jnp.dot(trailing, own_cols, precision=highest), "col")
    full_product = lax.all_gather(row_product, "row", axis=0, tiled=True)
    col_product = lax.dynamic_slice_in_dim(full_product, col_index * local_cols, local_cols, 0)
    corner = lax.psum(jnp.dot(own_cols.T, col_product, precision=highest), "col")
    small = jnp.dot(jnp.dot(block.T, corner, precision=highest), block, precision=highest)
    update_rows = jnp.dot(row_product, block, precision=highest) - 0.5 * jnp.dot(
        vectors, small, precision=highest
    )
    update_cols = jnp.dot(col_product, block, precision=highest) - 0.5 * jnp.dot(
        own_cols, small, precision=highest
    )
    reduced = (
        trailing
        - jnp.dot(vectors, update_cols.T, precision=highest)
        - jnp.dot(update_rows, own_cols.T, precision=highest)
    )
    return (reduced, vectors)


def solution(mesh):
    in_specs = (P("row", "col"),)
    out_specs = (P("row", "col"), P("row", None))
    return jax.shard_map(local, mesh=mesh, in_specs=in_specs, out_specs=out_specs, check_vma=False)
```

profile of v0, /device:TPU:1, one launch (start us, length us, event | category | flops | bytes accessed | tf_op | source)
XLA Modules:
  0.0 822.7 jit_solution(6686909799415139122)
XLA Ops:
  7.3 1.0 slice.3
  8.4 1.3 fusion.51
  9.6 1.2 fusion.49
  10.9 125.5 %all-reduce = (f32[64,64]{1,0:T(8,128)S(1)}, f32[64,64]{1,0:T(8,128)S(1)}) all-reduce(f32[64,64]{1,0:T(8,128)S(1)} %fusion.51, f32[64,64]{1,0:T(8,128)S(1)} %fusion.49), channel_id=1, replica_groups=mesh['row'=32,'col'=4] {'row'}, use_global_device_ids=true, to_apply=%region_0.1 | all-reduce | flops 8192 | bytes 65536 | tf_op jit(solution)/shard_map/psum | solution.py:70
  136.6 301.7 %while.39 = (s32[]{:T(128)}, f32[512,64]{0,1:T(8,128)S(1)}, f32[512,64]{1,0:T(8,128)S(1)}, f32[64]{0:T(128)S(1)}, f32[64,64]{0,1:T(8,128)S(1)}, /*index=5*/f32[6...) while((s32[]{:T(128)}, f32[512,64]{0,1:T(8,128)S(1)}, ...), condition=%wide.region_3.4_spmd.clone.clone, body=%wide.region_2.3_spmd.clone.clone.sunk | while | flops 231244 | bytes 613214 | solution.py:90
  439.2 40.4 %all-reduce.5.cloned.1.call-done = f32[512,64]{0,1:T(8,128)} async-done(((f32[512,64]{0,1:T(8,128)}), f32[512,64]{0,1:T(8,128)}) %all-reduce.5.cloned.1.call-update) | async-done | bytes 131088 | tf_op jit(solution)/shard_map/psum | solution.py:14
  479.6 51.9 %all-gather.3.cloned.1.call-done = f32[16384,64]{0,1:T(8,128)} async-done(((f32[512,64]{0,1:T(8,128)}), f32[16384,64]{0,1:T(8,128)}) %all-gather.3.cloned.1.call-update) | async-done | bytes 4194320 | tf_op jit(solution)/shard_map/all_gather | solution.py:92
  531.5 12.4 %convolution_bitcast_fusion.2 = f32[512,64]{0,1:T(8,128)} fusion(f32[512,4096]{1,0:T(8,128)} %param.5, f32[16384,64]{0,1:T(8,128)} %all-gather.3.cloned.1.call-done, s32[]{:T(128)S(6)} %select_n.289), kind=kOutput, calls=%fused_computation.64 | convolution fusion | flops 1610612736 | bytes 9568260 | tf_op jit(solution)/shard_map/dot_general | solution.py:96
  544.2 37.8 %all-reduce.7.cloned.1.call-done = f32[512,64]{0,1:T(8,128)} async-done(((f32[512,64]{0,1:T(8,128)}), f32[512,64]{0,1:T(8,128)}) %all-reduce.7.cloned.1.call-update) | async-done | bytes 131088 | tf_op jit(solution)/shard_map/psum | solution.py:96
  582.0 6.9 fusion.68
  589.0 44.5 %all-gather.5.cloned.1.call-done = f32[16384,64]{0,1:T(8,128)} async-done(((f32[512,64]{0,1:T(8,128)}), f32[16384,64]{0,1:T(8,128)}) %all-gather.5.cloned.1.call-update) | async-done | bytes 4194320 | tf_op jit(solution)/shard_map/all_gather | solution.py:97
  633.5 2.5 fusion.40
  636.0 13.5 %all-reduce.1 = (f32[64]{0:T(128)S(1)}, f32[64,64]{1,0:T(8,128)S(1)}) all-reduce(f32[64]{0:T(128)S(1)} %broadcast_select_fusion.2, f32[64,64]{1,0:T(8,128)S(1)} %fusion.40), channel_id=1, replica_groups=mesh['row'=32,'col'=4] {'col'}, use_global_device_ids=true, to_apply=%region_6.7 | all-reduce | flops 4160 | bytes 33280 | tf_op jit(solution)/shard_map/psum | solution.py:14
  649.5 137.0 %while.40 = (s32[]{:T(128)}, f32[64,64]{1,0:T(8,128)S(1)}, f32[64]{0:T(128)S(1)}, f32[64,64]{0,1:T(8,128)S(1)}, s32[]{:T(128)}, /*index=5*/s32[]{:T(128)}) while((s32[]{:T(128)}, f32[64,64]{1,0:T(8,128)S(1)}, f32[64]{0:T(128)S(1)}, f32[64,64]{0,1:T(8,128)S(1)}, s32[]{:T(128)}, /*index=5*/s32[]{:T(128)}) %tuple.100), condition=%wide.region_8.9_spmd.clone.clone, body=%wide.region_7.8_spmd.clone.clone.sunk | while | flops 61828 | bytes 69363 | solution.py:51
  650.8 0.8 fusion.104
  657.2 0.8 fusion.104
  663.6 0.8 fusion.104
  667.9 0.8 fusion.104
  670.1 0.8 fusion.104
  674.3 0.8 fusion.104
  680.8 0.8 fusion.104
  685.1 0.8 fusion.104
  687.2 0.8 fusion.104
  691.5 0.8 fusion.104
  697.9 0.8 fusion.104
  704.3 0.8 fusion.104
  708.6 0.8 fusion.104
  710.7 0.8 fusion.104
  715.0 0.8 fusion.104
  721.5 0.8 fusion.104
  725.7 0.8 fusion.104
  727.9 0.8 fusion.104
  732.2 0.8 fusion.104
  738.6 0.8 fusion.104
  745.0 0.8 fusion.104
  749.3 0.8 fusion.104
  751.4 0.8 fusion.104
  755.7 0.8 fusion.104
  762.1 0.8 fusion.104
  766.4 0.8 fusion.104
  768.6 0.8 fusion.104
  772.8 0.8 fusion.104
  779.3 0.8 fusion.104
  785.7 0.8 fusion.104
  787.0 4.7 fusion.42
  792.3 4.8 fusion.38
  797.8 8.3 %fusion.44 = f32[512,4096]{1,0:T(8,128)S(1)} fusion(f32[512,64]{1,0:T(8,128)S(1)} %fusion.39, f32[16384,64]{0,1:T(8,128)} %all-gather.3.cloned.1.call-done, s32[]{:T(128)S(6)} %select_n.289), kind=kOutput, calls=%fused_computation.69 | convolution fusion | flops 1610612736 | bytes 9568260 | tf_op jit(solution)/shard_map/dot_general | solution.py:110
  806.1 9.4 %subtract_subtract_fusion = f32[512,4096]{1,0:T(8,128)} fusion(f32[512,4096]{1,0:T(8,128)S(1)} %fusion.44, f32[512,4096]{1,0:T(8,128)S(1)} %bitcast.116, f32[512,64]{0,1:T(8,128)S(1)} %copy-done, f32[4096,64]{1,0:T(8,128)S(1)} %fusion.38), kind=kOutput, calls=%fused_computation.59 | convolution fusion | flops 1614807040 | bytes 26345472 | tf_op jit(solution)/shard_map/dot_general | solution.py:109
  (1028 shorter events, 202.6 us)
Async XLA Ops:
  7.2 472.4 %all-reduce.5.cloned.1.call-start = ((), (), s32[]{:S(2)}) async-start(), calls=%async_computation | async-start | bytes 262144 | tf_op jit(solution)/shard_map/psum | solution.py:14
  439.1 92.4 %all-gather.3.cloned.1.call-start = ((), (), s32[]{:S(2)}) async-start(), calls=%async_computation.1 | async-start | bytes 4325376 | tf_op jit(solution)/shard_map/all_gather | solution.py:92
  479.6 102.4 %all-reduce.7.cloned.1.call-start = ((), (), s32[]{:S(2)}) async-start(), calls=%async_computation.2 | async-start | bytes 262144 | tf_op jit(solution)/shard_map/psum | solution.py:96
  543.9 89.6 %all-gather.5.cloned.1.call-start = ((), (), s32[]{:S(2)}) async-start(), calls=%async_computation.3 | async-start | bytes 4325376 | tf_op jit(solution)/shard_map/all_gather | solution.py:97
  589.0 202.8 %copy-start.1 = (f32[512,64]{0,1:T(8,128)S(1)}, f32[512,64]{0,1:T(8,128)}, u32[]{:S(2)}) copy-start(f32[512,64]{0,1:T(8,128)} %all-reduce.7.cloned.1.call-done) | copy-start | bytes 393220
  787.0 10.2 %copy-start = (f32[512,64]{0,1:T(8,128)S(1)}, f32[512,64]{0,1:T(8,128)}, u32[]{:S(2)}) copy-start(f32[512,64]{0,1:T(8,128)} %all-reduce.5.cloned.1.call-done) | copy-start | bytes 393220
  792.3 13.8 %slice-start = ((s8[8388608]{0:T(1024)(128)(4,1)}), s8[4194304]{0:T(1024)(128)(4,1)S(1)}, s32[]{:S(2)}) async-start(s8[8388608]{0:T(1024)(128)(4,1)} %bitcast.115), calls=%async_computation.4 | async-start | bytes 8388608
  797.8 8.3 %slice-start.1 = ((s8[8388608]{0:T(1024)(128)(4,1)}), s8[4194304]{0:T(1024)(128)(4,1)S(1)}, s32[]{:S(2)}) async-start(s8[8388608]{0:T(1024)(128)(4,1)} %bitcast.115), calls=%async_computation.5 | async-start | bytes 8388608
Sparse Core Ops, SparseCore 0:
  439.2 40.2 all-reduce.4
  482.1 49.3 all-gather.2
  544.1 37.8 all-reduce.6
  584.1 49.3 all-gather.4
where the time goes:
time: 829 us; the launch traced here: 823 us
  loops' own time  216 us (26%)
  waiting for transfers between devices  175 us (21%)
  blocking collectives  139 us (17%)
  local copies, waits for them, and re-layouts  122 us (15%)
  matrix products  113 us (14%)
  other arithmetic  43.2 us (5%)
  between operations  14 us (2%)
    another operation x1, loops' own time, local(): lax.fori_loop(0, NB, body_turn, start + (top_rows,))  174 us
    psum x1, blocking collectives, local(): panel_gram, top_rows = lax.psum((local_gram, local_top), 'row')  126 us
    all_gather x1, waiting for transfers between devices, local(): every_row = lax.all_gather(vectors, 'row', axis=0, tiled=True)  51.9 us
    dot_general x64, matrix products, block_turn(): column = -factor * jnp.dot(block, prior, precision=highest)  50.3 us
    all_gather x1, waiting for transfers between devices, local(): full_product = lax.all_gather(row_product, 'row', axis=0, tiled=True)  44.5 us
    another operation x1, loops' own time, block_factor(): lax.fori_loop(0, width, block_turn, jnp.zeros((width, width), jnp.float32))  42.3 us
    dynamic_slice x64, local copies, waits for them, and re-layouts, reflect_column(): leading = pivot_row[step_col]  41.7 us
    dynamic_slice x64, local copies, waits for them, and re-layouts, reflect_column(): norm_sq = col_dots[step_col]  41.1 us
  transfers between devices with their start and end apart: 4, of which 4 were waited for; matrix products, arithmetic and copies ran while one was open for 1% of the time, Pallas kernels for 0%

commit v1 on v0

v1 whole, which is shorter than its diff:
```python
import functools

import jax
import jax.numpy as jnp
from jax import lax
from jax.experimental import pallas as pl
from jax.experimental.pallas import tpu as pltpu
from jax.sharding import PartitionSpec as P

NB = 64
SIDE = 4
MESH = pl.DeviceIdType.MESH
HIGHEST = lax.Precision.HIGHEST
NN = (((1,), (0,)), ((), ()))
NT = (((1,), (1,)), ((), ()))


def dot(a, b, dims=NN):
    return lax.dot_general(a, b, dims, precision=HIGHEST, preferred_element_type=jnp.float32)


def dot16(a, b, dims=NN):
    return lax.dot_general(a, b, dims, preferred_element_type=jnp.float32)


def split(a):
    high = a.astype(jnp.bfloat16)
    return high, (a - high.astype(jnp.float32)).astype(jnp.bfloat16)


def wrap(i):
    return lax.rem(i, SIDE)


class Ids:
    def __init__(self):
        self.count = 0

    def take(self, n):
        first = self.count
        self.count += n
        return first


IDS = Ids()
HOME = IDS.take(4)
ROWS = IDS.take(4)
GATHER_P = IDS.take(20)
GATHER_Y = IDS.take(20)
GRAM = IDS.take(4)
CORNER = IDS.take(4)
REDUCE = IDS.take(4)
YROWS = IDS.take(4)
COUNT = IDS.count


def factor(gt, r_ref):
    lanes = lax.broadcasted_iota(jnp.int32, (8, 128), 1)
    subs = lax.broadcasted_iota(jnp.int32, (8, 128), 0)
    square = jnp.concatenate([gt, jnp.zeros_like(gt)], axis=0)
    t_all = jnp.transpose(square)[NB:, :]
    S, T, C = [], [], []
    for b in range(8):
        rows = slice(8 * b, 8 * b + 8)
        unit = jnp.where(lanes == subs + (8 * b + NB), 1.0, 0.0)
        S.append(jnp.where(lanes < NB, gt[rows], unit))
        T.append(jnp.where(lanes < NB, t_all[rows], unit))
        C.append(jnp.where(lanes == subs + 8 * b, 1.0, 0.0))
    lane_row = lax.broadcasted_iota(jnp.int32, (1, 128), 1)
    for j in range(NB):
        b, s = j // 8, j % 8
        srow, trow = S[b][s : s + 1, :], T[b][s : s + 1, :]
        d, a = srow[:, j : j + 1], trow[:, j : j + 1]
        length = jnp.sqrt(d)
        lead = jnp.where(a >= 0.0, -length, length)
        rrow = jnp.where(lane_row >= j, srow, 0.0) * (1.0 / lead)
        r_ref[NB + j : NB + j + 1, :] = rrow
        urow = jnp.where(lane_row < NB, jnp.where(lane_row >= j, trow - rrow, 0.0), trow)
        pivot_inv = 1.0 / (a - lead)
        d_inv = 1.0 / d
        later = lane_row > j
        surow = jnp.where(later, srow, 0.0) * d_inv
        turow = jnp.where(later, urow, 0.0) * pivot_inv
        for m in range(b, 8):
            scol, tcol = S[m][:, j : j + 1], T[m][:, j : j + 1]
            ds, dt = scol * surow, tcol * turow
            if m == b:
                ds, dt = jnp.where(subs > s, ds, 0.0), jnp.where(subs > s, dt, 0.0)
            S[m] = S[m] - ds
            T[m] = T[m] - dt
        for m in range(b + 1):
            ccol = C[m][:, j : j + 1]
            C[m] = jnp.where(lanes == j, ccol * pivot_inv, C[m] - ccol * jnp.where(lane_row < NB, turow, 0.0))
    return jnp.concatenate(C, axis=0), jnp.concatenate(T, axis=0)


def kernel(
    a_hbm, x_out, z_out,
    a_v, head, head_t, pbuf, ybuf, prow, yrow, part, rbuf, gbuf, cbuf, r_ref, h_ref,
    load_sem, send, recv,
):
    r, x = lax.axis_index("row"), lax.axis_index("col")
    z, y, k = r // 8, lax.rem(r // 2, SIDE), lax.rem(r, 2)
    lanes64 = lax.broadcasted_iota(jnp.int32, (NB, 128), 1)

    def dev(z_, y_, k_, x_):
        return (z_ * 8 + y_ * 2 + k_, x_)

    def remote(src, dst, s, t, device):
        return pltpu.make_async_remote_copy(
            src_ref=src, dst_ref=dst, send_sem=send.at[s], recv_sem=recv.at[t],
            device_id=device, device_id_type=MESH,
        )

    sibling = dev(z, y, 1 - k, x)
    whole = pltpu.make_async_copy(a_hbm, a_v, load_sem.at[0])
    first = pltpu.make_async_copy(a_hbm.at[:, pl.ds(0, 128)], head, load_sem.at[1])
    owns = x == 0

    @pl.when(owns)
    def _():
        first.start()

    whole.start()

    barrier = pltpu.get_barrier_semaphore()
    peers = [dev(wrap(z + i), y, k, wrap(x + j)) for i in range(SIDE) for j in range(SIDE) if i or j]
    peers += [dev(z, wrap(y + i), k, x) for i in range(1, SIDE)] + [sibling]
    for peer in peers:
        pl.semaphore_signal(barrier, inc=1, device_id=peer, device_id_type=MESH)

    r_ref[0:NB, :] = jnp.zeros((NB, 128), jnp.float32)

    @pl.when(owns)
    def _():
        first.wait()
        head_t[...] = jnp.transpose(head[...])

        @pl.when(r == 0)
        def _():
            head_t[0:NB, 0:128] = jnp.where(lanes64 >= NB, head_t[0:NB, 0:128], 0.0)

    pl.semaphore_wait(barrier, len(peers))

    def home_piece(q):
        return head_t.at[pl.ds(0, NB), pl.ds(q * 128, 128)]

    def home_copy(q):
        return remote(home_piece(q), pbuf.at[k, y, q], HOME + q, HOME, dev(q, y, k, z))

    self_home = owns & (r // 8 == 0)
    local_home = pltpu.make_async_copy(home_piece(0), pbuf.at[k, y, 0], load_sem.at[2])

    def rows_copy(d):
        return remote(head_t.at[pl.ds(0, NB)], prow, ROWS + d, ROWS, dev(z, y, k, d))

    local_rows = pltpu.make_async_copy(head_t.at[pl.ds(0, NB)], prow, load_sem.at[3])

    @pl.when(owns)
    def _():
        @pl.when(z == 0)
        def _():
            local_home.start()

        @pl.when(z != 0)
        def _():
            home_copy(0).start()

        for q in range(1, SIDE):
            home_copy(q).start()
        for d in range(1, SIDE):
            rows_copy(d).start()
        local_rows.start()

    @pl.when(self_home)
    def _():
        local_home.wait()

    @pl.when(jnp.logical_not(self_home))
    def _():
        remote(pbuf.at[k, y, z], pbuf.at[k, y, z], HOME, HOME, sibling).wait_recv()

    low, high = pl.ds(0, NB // 2), pl.ds(NB // 2, NB // 2)

    def gather(buf, base):
        sends = []

        def go(src, slot, device):
            copy = remote(src, src, base + slot, base + slot, device)
            copy.start()
            sends.append(copy)

        def came(dst, slot):
            remote(dst, dst, base + slot, base + slot, sibling).wait_recv()

        for d in range(1, SIDE):
            go(buf.at[k, y, z, low], d - 1, dev(wrap(z + d), y, k, x))
            go(buf.at[k, y, z, high], 3 + d - 1, dev(z, wrap(y + d), k, x))
        for d in range(1, SIDE):
            came(buf.at[k, y, wrap(z + SIDE - d), low], d - 1)
        for d in range(1, SIDE):
            go(buf.at[k, y, :, low], 6 + d - 1, dev(z, wrap(y + d), k, x))
        for d in range(1, SIDE):
            came(buf.at[k, wrap(y + SIDE - d), z, high], 3 + d - 1)
        for d in range(1, SIDE):
            go(buf.at[k, :, z, high], 9 + d - 1, dev(wrap(z + d), y, k, x))
        go(buf.at[k, y, :, low], 12, sibling)
        go(buf.at[k, :, z, high], 16, sibling)
        for d in range(1, SIDE):
            came(buf.at[k, wrap(y + SIDE - d), :, low], 6 + d - 1)
            go(buf.at[k, wrap(y + SIDE - d), :, low], 12 + d, sibling)
            came(buf.at[k, :, wrap(z + SIDE - d), high], 9 + d - 1)
            go(buf.at[k, :, wrap(z + SIDE - d), high], 16 + d, sibling)
        for d in range(SIDE):
            came(buf.at[1 - k, wrap(y + SIDE - d), :, low], 12 + d)
            came(buf.at[1 - k, :, wrap(z + SIDE - d), high], 16 + d)
        return sends

    sends = gather(pbuf, GATHER_P)

    def wide(buf, m):
        return jnp.concatenate([buf[m % 2, m // 2, q] for q in range(SIDE)], axis=1)

    gram = jnp.zeros((NB, NB), jnp.float32)
    for m in range(8):
        piece = wide(pbuf, m)
        gram = gram + dot(piece, piece, NT)
    top = jnp.where(owns, pbuf[0, 0, 0], 0.0)
    gbuf[x] = jnp.where(lanes64 < NB, jnp.concatenate([gram, gram], axis=1), top)

    def exchange(buf, base):
        for d in range(1, SIDE):
            copy = remote(buf.at[x], buf.at[x], base + d, base + d, dev(z, y, k, wrap(x + d)))
            copy.start()
            sends.append(copy)

    def exchanged(buf, base):
        for d in range(1, SIDE):
            there = buf.at[wrap(x + SIDE - d)]
            remote(there, there, base + d, base + d, sibling).wait_recv()
        return (buf[0] + buf[1]) + (buf[2] + buf[3])

    exchange(gbuf, GRAM)

    whole.wait()
    acc = jnp.zeros((2 * NB, a_v.shape[0]), jnp.float32)
    for m in range(8):
        p_hi, p_lo = split(wide(pbuf, m))
        both = jnp.concatenate([p_hi, p_lo], axis=0)
        a_hi, a_lo = split(a_v[:, m * 512 : (m + 1) * 512])
        acc = acc + (dot16(both, a_hi, NT) + dot16(both, a_lo, NT))
    part[...] = acc[:NB] + acc[NB:]

    gt = exchanged(gbuf, GRAM)
    m_all, t_all = factor(gt, r_ref)
    m_t = jnp.transpose(jnp.concatenate([m_all, jnp.zeros_like(m_all)], axis=0))[:NB, :]
    r_all = r_ref[...]
    r_shift = jnp.transpose(r_all)[:NB, :]
    k_t = -dot(t_all[:, NB:], r_all[NB:, NB:])

    @pl.when(owns)
    def _():
        part[...] = part[...] - dot(r_shift[:, NB:], head_t[NB : 2 * NB, :])

    def piece_of(q):
        return part.at[:, pl.ds(pl.multiple_of(q * 128, 128), 128)]

    def reduce_copy(d):
        q = wrap(z + d)
        return remote(piece_of(q), rbuf.at[x], REDUCE + d, REDUCE + x, dev(q, y, k, z))

    diagonal = x == z
    local_reduce = pltpu.make_async_copy(piece_of(z), rbuf.at[x], load_sem.at[4])

    @pl.when(diagonal)
    def _():
        local_reduce.start()

    @pl.when(jnp.logical_not(diagonal))
    def _():
        reduce_copy(0).start()

    for d in range(1, SIDE):
        reduce_copy(d).start()

    def reduce_came(d):
        there = rbuf.at[wrap(x + d)]
        remote(there, there, REDUCE, REDUCE + wrap(x + d), sibling).wait_recv()

    for d in range(1, SIDE):
        reduce_came(d)

    @pl.when(diagonal)
    def _():
        local_reduce.wait()

    @pl.when(jnp.logical_not(diagonal))
    def _():
        reduce_came(0)

    ybuf[k, y, z] = (rbuf[0] + rbuf[1]) + (rbuf[2] + rbuf[3])

    def yrows_copy(d):
        return remote(ybuf.at[k, y, z], yrow.at[z], YROWS + d, YROWS + z, dev(x, y, k, wrap(x + d)))

    local_yrows = pltpu.make_async_copy(ybuf.at[k, y, z], yrow.at[z], load_sem.at[5])

    @pl.when(diagonal)
    def _():
        local_yrows.start()

    @pl.when(jnp.logical_not(diagonal))
    def _():
        yrows_copy(0).start()

    for d in range(1, SIDE):
        yrows_copy(d).start()

    sends += gather(ybuf, GATHER_Y)

    shift_c = jnp.where(owns, r_shift, 0.0)
    corner = jnp.zeros((NB, NB), jnp.float32)
    for m in range(8):
        piece = wide(pbuf, m)
        if m == 0:
            piece = jnp.concatenate([piece[:, :128] - shift_c, piece[:, 128:]], axis=1)
        corner = corner + dot(piece, wide(ybuf, m), NT)
    cbuf[x] = jnp.concatenate([corner, jnp.zeros_like(corner)], axis=1)
    exchange(cbuf, CORNER)
    corner = exchanged(cbuf, CORNER)[:, :NB]
    small = dot(dot(k_t, corner), k_t, NT)
    mt = m_t[:, :NB]
    zero = jnp.zeros((NB, NB), jnp.float32)
    h_ref[:NB, :] = jnp.concatenate([-0.5 * dot(small, mt), k_t], axis=1)
    h_ref[NB:, :] = jnp.concatenate([mt, zero], axis=1)
    h = h_ref[...]

    for m in range(8):
        piece = wide(pbuf, m)
        if m == 0:
            piece = jnp.concatenate([piece[:, :128] - shift_c, piece[:, 128:]], axis=1)
        both = jnp.concatenate([piece, wide(ybuf, m)], axis=0)
        z_out[:, m * 512 : (m + 1) * 512] = dot(h, both)

    for d in range(1, SIDE):
        q = wrap(z + d)
        remote(yrow.at[q], yrow.at[q], YROWS, YROWS + q, sibling).wait_recv()

    @pl.when(diagonal)
    def _():
        local_yrows.wait()

    @pl.when(jnp.logical_not(diagonal))
    def _():
        remote(yrow.at[z], yrow.at[z], YROWS, YROWS + z, sibling).wait_recv()

    @pl.when(owns)
    def _():
        local_rows.wait()

    @pl.when(jnp.logical_not(owns))
    def _():
        remote(prow, prow, ROWS, ROWS, sibling).wait_recv()

    piece = prow[...]
    shift_r = jnp.where(r == 0, r_shift, 0.0)
    piece = jnp.concatenate([piece[:, :128] - shift_r, piece[:, 128:]], axis=1)
    both = jnp.concatenate([piece] + [jnp.concatenate([yrow[q] for q in range(SIDE)], axis=1)], axis=0)
    uv = dot(h, both)
    x_out[...] = jnp.transpose(jnp.concatenate([uv[NB:], uv[:NB]], axis=0))

    @pl.when(owns)
    def _():
        @pl.when(z != 0)
        def _():
            home_copy(0).wait_send()

        for q in range(1, SIDE):
            home_copy(q).wait_send()
        for d in range(1, SIDE):
            rows_copy(d).wait_send()

    @pl.when(jnp.logical_not(diagonal))
    def _():
        reduce_copy(0).wait_send()
        yrows_copy(0).wait_send()

    for d in range(1, SIDE):
        reduce_copy(d).wait_send()
        yrows_copy(d).wait_send()
    for copy in sends:
        copy.wait_send()


def update_kernel(a_ref, x_ref, z_ref, out_ref, v_ref):
    x_hi, x_lo = split(x_ref[...])
    z_hi, z_lo = split(z_ref[...])
    out_ref[...] = a_ref[...] - ((dot16(x_lo, z_hi) + dot16(x_hi, z_lo)) + dot16(x_hi, z_hi))
    v_ref[...] = x_ref[:, :NB]


def local(trailing):
    rows, cols = trailing.shape
    f32 = jnp.float32
    x_mat, z_mat = pl.pallas_call(
        kernel,
        out_shape=(jax.ShapeDtypeStruct((rows, 128), f32), jax.ShapeDtypeStruct((128, cols), f32)),
        in_specs=[pl.BlockSpec(memory_space=pl.ANY)],
        out_specs=(pl.BlockSpec(memory_space=pltpu.VMEM), pl.BlockSpec(memory_space=pltpu.VMEM)),
        scratch_shapes=[
            pltpu.VMEM((rows, cols), f32),
            pltpu.VMEM((rows, 128), f32),
            pltpu.VMEM((128, rows), f32),
            pltpu.VMEM((2, SIDE, SIDE, NB, 128), f32),
            pltpu.VMEM((2, SIDE, SIDE, NB, 128), f32),
            pltpu.VMEM((NB, rows), f32),
            pltpu.VMEM((SIDE, NB, 128), f32),
            pltpu.VMEM((NB, rows), f32),
            pltpu.VMEM((SIDE, NB, 128), f32),
            pltpu.VMEM((SIDE, NB, 128), f32),
            pltpu.VMEM((SIDE, NB, 128), f32),
            pltpu.VMEM((128, 128), f32),
            pltpu.VMEM((128, 128), f32),
            pltpu.SemaphoreType.DMA((6,)),
            pltpu.SemaphoreType.DMA((COUNT,)),
            pltpu.SemaphoreType.DMA((COUNT,)),
        ],
        compiler_params=pltpu.CompilerParams(
            collective_id=0, has_side_effects=True, vmem_limit_bytes=40 * 2**20
        ),
    )(trailing)
    step = 64
    return pl.pallas_call(
        update_kernel,
        grid=(rows // step,),
        out_shape=(jax.ShapeDtypeStruct((rows, cols), f32), jax.ShapeDtypeStruct((rows, NB), f32)),
        in_specs=[
            pl.BlockSpec((step, cols), lambda i: (i, 0)),
            pl.BlockSpec((step, 128), lambda i: (i, 0)),
            pl.BlockSpec((128, cols), lambda i: (0, 0)),
        ],
        out_specs=(pl.BlockSpec((step, cols), lambda i: (i, 0)), pl.BlockSpec((step, NB), lambda i: (i, 0))),
        compiler_params=pltpu.CompilerParams(vmem_limit_bytes=40 * 2**20),
    )(trailing, x_mat, z_mat)


def solution(mesh):
    return jax.shard_map(
        local, mesh=mesh, in_specs=(P("row", "col"),), out_specs=(P("row", "col"), P("row", None)), check_vma=False
    )
```

time: 829 us -> 79.8 us (0.10)
  loops' own time: 216 us -> 0 us
  waiting for transfers between devices: 175 us -> 0 us
  blocking collectives: 139 us -> 0 us
  local copies, waits for them, and re-layouts: 122 us -> 4.15 us
  matrix products: 113 us -> 0 us
  Pallas kernels: 0 us -> 74.9 us
  other arithmetic: 43.2 us -> 0 us
  between operations: 14 us -> 0.65 us
    another operation x2 -> x0, loops' own time: 216 us -> none  [the longest x1 174 us: local(): lax.fori_loop(0, NB, body_turn, start + (top_rows,))]
    psum x2 -> x0, blocking collectives: 139 us -> none  [the longest x1 126 us: local(): panel_gram, top_rows = lax.psum((local_gram, local_top), 'row')]
    dynamic_slice x192 -> x0, local copies, waits for them, and re-layouts: 120 us -> none  [the longest x64 41.7 us: reflect_column(): leading = pivot_row[step_col]]
    dot_general x141 -> x0, matrix products: 113 us -> none  [the longest x64 50.3 us: block_turn(): column = -factor * jnp.dot(block, prior, precision=highest)]
    all_gather x2 -> x0, waiting for transfers between devices: 96.4 us -> none  [the longest x1 51.9 us: local(): every_row = lax.all_gather(vectors, 'row', axis=0, tiled=True)]
    psum x2 -> x0, waiting for transfers between devices: 78.2 us -> none  [the longest x1 40.4 us: from_root(): return lax.psum(jnp.where(mine, array, jnp.zeros_like(array)), axis)]
    pallas_call x0 -> x2, Pallas kernels: none -> 74.9 us  [the longest x1 67.5 us: local(): pl.pallas_call(kernel, out_shape=(jax.ShapeDtypeStruct((rows, 128), f32),...]
    select_n x323 -> x0, other arithmetic: 26.6 us -> none  [the longest x128 11 us: reflect_column(): jnp.where((columns == step_col)[None, :], new_column[:, None], panel_cols)]
  transfers between devices with their start and end apart: 4 -> 0, of which waited for: 4 -> 0; matrix products, arithmetic and copies ran while one was open for 1% -> 0% of each run, Pallas kernels for 0% -> 0%
where the time goes in v1:
time: 79.8 us; the launch traced here: 79.7 us
  Pallas kernels  74.9 us (94%)
  local copies, waits for them, and re-layouts  4.15 us (5%)
    pallas_call x1, Pallas kernels, local(): pl.pallas_call(kernel, out_shape=(jax.ShapeDtypeStruct((rows, 128), f32),...  67.5 us
    pallas_call x1, Pallas kernels, local(): pl.pallas_call(update_kernel, grid=(rows // step,), out_shape=(jax.ShapeD...  7.35 us
    unnamed x2, local copies, waits for them, and re-layouts  3.37 us

profile of v1, /device:TPU:1, one launch (start us, length us, event | category | flops | bytes accessed | tf_op | source)
XLA Modules:
  0.0 79.7 jit_solution(1646789960231937974)
XLA Ops:
  0.6 0.0 copy-start
  0.6 3.4 %copy-done = f32[512,4096]{1,0:T(8,128)S(1)} copy-done((f32[512,4096]{1,0:T(8,128)S(1)}, f32[512,4096]{1,0:T(8,128)}, u32[]{:S(2)}) %copy-start) | copy-done | bytes 8388632
  4.0 67.5 %shard_map.30 = (f32[512,128]{1,0:T(8,128)S(1)}, f32[128,4096]{1,0:T(8,128)S(1)}) custom-call(f32[512,4096]{1,0:T(8,128)S(1)} %copy-done), custom_call_target="tpu_custom_call" | custom-call | tf_op jit(solution)/shard_map/pallas_call | solution.py:405
  71.5 7.3 %shard_map.31 = (f32[512,4096]{1,0:T(8,128)}, f32[512,64]{1,0:T(8,128)S(1)}) custom-call(f32[512,4096]{1,0:T(8,128)S(1)} %copy-done, f32[512,128]{1,0:T(8,128)S(1)} %get-tuple-element.4.x_ref, f32[128,4096]{1,0:T(8,128)S(1)} %get-tuple-element.5.z_ref), custom_call_target="tpu_custom_call" | custom-call | tf_op jit(solution)/shard_map/pallas_call | solution.py:433
  78.9 0.8 copy.3
Async XLA Ops:
  0.6 3.4 %copy-start = (f32[512,4096]{1,0:T(8,128)S(1)}, f32[512,4096]{1,0:T(8,128)}, u32[]{:S(2)}) copy-start(f32[512,4096]{1,0:T(8,128)} %a_ref.1) | copy-start | bytes 25165828

commit v2 on v0

v2 whole, which is shorter than its diff:
```python
import jax
import jax.numpy as jnp
from jax import lax
from jax.experimental import pallas as pl
from jax.experimental.pallas import tpu as pltpu
from jax.sharding import PartitionSpec as P

NB = 64
SIDE = 4
MESH = pl.DeviceIdType.MESH
HIGHEST = lax.Precision.HIGHEST
NN = (((1,), (0,)), ((), ()))
NT = (((1,), (1,)), ((), ()))
TN = (((0,), (0,)), ((), ()))


def dot(a, b, dims=NN):
    return lax.dot_general(a, b, dims, precision=HIGHEST, preferred_element_type=jnp.float32)


def dot16(a, b, dims=NN):
    return lax.dot_general(a, b, dims, preferred_element_type=jnp.float32)


def split(a):
    high = a.astype(jnp.bfloat16)
    return high, (a - high.astype(jnp.float32)).astype(jnp.bfloat16)


def split3(a):
    high = a.astype(jnp.bfloat16)
    rest = a - high.astype(jnp.float32)
    middle = rest.astype(jnp.bfloat16)
    return high, middle, (rest - middle.astype(jnp.float32)).astype(jnp.bfloat16)


def stack(parts):
    return jnp.concatenate(parts, axis=0)


def wrap(i):
    return lax.rem(i, SIDE)


AROUND = [(2, 2), (2, 1), (2, 3), (1, 2), (3, 2), (1, 1), (3, 3), (1, 3), (3, 1), (2, 0), (0, 2), (1, 0), (3, 0), (0, 1), (0, 3)]


class Ids:
    def __init__(self):
        self.count = 0

    def take(self, n):
        first = self.count
        self.count += n
        return first


IDS = Ids()
ROWS = IDS.take(4)
HOME = IDS.take(4)
GRAM = IDS.take(4)
SPREAD = IDS.take(17)
HALVES = IDS.take(4)
SCATTER = IDS.take(16)
GATHER = IDS.take(20)
OWN_ROWS = IDS.take(4)
CORNER = IDS.take(4)
COUNT = IDS.count


def factor(gt, r_ref, u_ref, out):
    lanes = lax.broadcasted_iota(jnp.int32, (8, 128), 1)
    subs = lax.broadcasted_iota(jnp.int32, (8, 128), 0)
    lane = lax.broadcasted_iota(jnp.int32, (1, 128), 1)
    t_all = jnp.transpose(stack([gt, jnp.zeros_like(gt)]))[NB:, :]
    S, T, C = [], [], []
    for b in range(8):
        rows = slice(8 * b, 8 * b + 8)
        unit = jnp.where(lanes == subs + (8 * b + NB), 1.0, 0.0)
        S.append(jnp.where(lanes < NB, gt[rows], unit))
        T.append(jnp.where(lanes < NB, t_all[rows], unit))
        C.append(jnp.where(lanes == subs + 8 * b, 1.0, 0.0))
    for j in range(NB):
        b, s = j // 8, j % 8
        srow, trow = S[b][s : s + 1, :], T[b][s : s + 1, :]
        d = jnp.broadcast_to(srow[:, j : j + 1], (1, 128))
        a = jnp.broadcast_to(trow[:, j : j + 1], (1, 128))
        root_inv = lax.rsqrt(d)
        positive = a >= 0.0
        pivot_inv = 1.0 / (jnp.abs(a) + d * root_inv)
        pivot_inv = jnp.where(positive, pivot_inv, -pivot_inv)
        rrow = jnp.where(lane >= j, srow, 0.0) * jnp.where(positive, -root_inv, root_inv)
        r_ref[NB + j : NB + j + 1, :] = rrow
        urow = jnp.where(lane < NB, jnp.where(lane >= j, trow - rrow, 0.0), trow)
        u_ref[j : j + 1, :] = urow
        later = lane > j
        surow = jnp.where(later, srow, 0.0) * (1.0 / d)
        turow = jnp.where(later, urow, 0.0) * pivot_inv
        for m in range(b, 8):
            scol, tcol = S[m][:, j : j + 1], T[m][:, j : j + 1]
            if m == b:
                below = subs[:, :1] > s
                scol, tcol = jnp.where(below, scol, 0.0), jnp.where(below, tcol, 0.0)
            S[m] = S[m] - scol * surow
            T[m] = T[m] - tcol * turow
        curow = jnp.where(lane < NB, jnp.where(lane == j, 1.0 - pivot_inv, turow), 0.0)
        for m in range(b + 1):
            C[m] = C[m] - C[m][:, j : j + 1] * curow
        if s == 7:
            if b == 7:
                out += [stack(C), stack(T)]
            yield


def kernel(
    a_hbm, a_v, x_out, z_out, vt_out,
    a_hi, a_lo, head, lead, panel, prow, pq, dbuf, sbuf, rbuf, wv, wv_rows, gbuf, gt_ref, cbuf, r_ref, u_ref,
    load_sem, send, recv,
):
    r, x = lax.axis_index("row"), lax.axis_index("col")
    z, y, k = r // 8, lax.rem(r // 2, SIDE), lax.rem(r, 2)
    lanes64 = lax.broadcasted_iota(jnp.int32, (NB, 128), 1)

    def dev(z_, y_, k_, x_):
        return (z_ * 8 + y_ * 2 + k_, x_)

    def remote(src, dst, s, t, device):
        return pltpu.make_async_remote_copy(
            src_ref=src, dst_ref=dst, send_sem=send.at[s], recv_sem=recv.at[t],
            device_id=device, device_id_type=MESH,
        )

    sends = []

    def launch(copy, when=None):
        if when is None:
            copy.start()
        else:
            pl.when(when)(copy.start)
        sends.append((copy, when))

    def finish():
        for copy, when in sends:
            if when is None:
                copy.wait_send()
            else:
                pl.when(when)(copy.wait_send)
        sends.clear()

    sibling = dev(z, y, 1 - k, x)

    def came(dst, slot):
        remote(dst, dst, slot, slot, sibling).wait_recv()

    owns = x == 0
    first_row = r == 0
    half = a_v.shape[0] // 2

    def head_load(q):
        rows = pl.ds(q * 128, 128)
        return pltpu.make_async_copy(a_hbm.at[rows, pl.ds(0, 128)], head.at[rows], load_sem.at[q])

    def load(i):
        rows = pl.ds(i * half, half)
        return pltpu.make_async_copy(a_hbm.at[rows], a_v.at[rows], load_sem.at[4 + i])

    lead_load = pltpu.make_async_copy(a_hbm.at[pl.ds(0, NB)], lead, load_sem.at[6])

    @pl.when(owns)
    def _():
        for q in range(SIDE):
            head_load(q).start()

    pl.when(first_row)(lead_load.start)
    barrier = pltpu.get_barrier_semaphore()
    peers = [dev(wrap(z + i), y, k, wrap(x + j)) for i in range(SIDE) for j in range(1, SIDE)]
    peers += [dev(wrap(z + i), wrap(y + j), k, x) for i, j in AROUND] + [sibling]
    for peer in peers:
        pl.semaphore_signal(barrier, inc=1, device_id=peer, device_id_type=MESH)

    load(0).start()
    load(1).start()
    r_ref[0:NB, :] = jnp.zeros((NB, 128), jnp.float32)

    @pl.when(owns)
    def _():
        for q in range(SIDE):
            head_load(q).wait()
            panel[q] = jnp.transpose(head[q * 128 : (q + 1) * 128, :])
            if q == 0:
                panel[0, 0:NB] = jnp.where(first_row & (lanes64 < NB), 0.0, panel[0, 0:NB])
            prow[:, q * 128 : (q + 1) * 128] = panel[q, 0:NB]

    pl.semaphore_wait(barrier, len(peers))

    for d in (2, 1, 3):
        launch(remote(prow, prow, ROWS + d, ROWS, dev(z, y, k, d)), owns)

    def home_copy(q):
        return remote(panel.at[q], pq, HOME + q, HOME, dev(q, y, k, z))

    self_home = owns & (z == 0)
    home_local = pltpu.make_async_copy(panel.at[0], pq, load_sem.at[7])
    pl.when(self_home)(home_local.start)
    launch(home_copy(0), owns & (z != 0))
    for q in range(1, SIDE):
        launch(home_copy(q), owns)

    def exchange(buf, base, when=None):
        for d in (2, 1, 3):
            launch(remote(buf.at[x], buf.at[x], base + d, base + d, dev(z, y, k, wrap(x + d))), when)

    def exchanged(buf, base):
        for d in range(1, SIDE):
            came(buf.at[wrap(x + SIDE - d)], base + d)
        return (buf[0] + buf[1]) + (buf[2] + buf[3])

    @pl.when(first_row)
    def _():
        lead_load.wait()
        lead[:, 0:128] = jnp.where(owns & (lanes64 < NB), 0.0, lead[:, 0:128])
        gram = jnp.zeros((3 * NB, 3 * NB), jnp.float32)
        for m in range(8):
            three = stack(split3(lead[:, m * 512 : (m + 1) * 512]))
            gram = gram + dot16(three, three, NT)
        gram = gram[:NB] + gram[NB : 2 * NB] + gram[2 * NB :]
        gram = gram[:, :NB] + gram[:, NB : 2 * NB] + gram[:, 2 * NB :]
        top = jnp.where(owns, lead[:, 0:128], 0.0)
        gbuf[x] = jnp.where(lanes64 < NB, jnp.concatenate([gram, gram], axis=1), top)

    exchange(gbuf, GRAM, first_row)

    def split_rows(part_id):
        load(part_id).wait()

        def body(step, carry):
            rows = pl.ds(pl.multiple_of(part_id * half + step * 16, 16), 16)
            for kk in range(2):
                for i in range(SIDE):
                    first = i * 1024 + kk * 512
                    a_hi[kk, i, rows, :], a_lo[kk, i, rows, :] = split(a_v[rows, first : first + 512])
            return carry

        lax.fori_loop(0, half // 16, body, 0)

    split_rows(0)
    split_rows(1)

    @pl.when(first_row)
    def _():
        gt_ref[...] = exchanged(gbuf, GRAM)

    launch(remote(gt_ref, gt_ref, SPREAD + 16, SPREAD, sibling), first_row)
    first_chip = (z == 0) & (y == 0)

    def gt_came():
        came(gt_ref, SPREAD)

    pl.when(first_chip & (k == 1))(gt_came)
    for i, j in AROUND:
        launch(remote(gt_ref, gt_ref, SPREAD + 4 * i + j, SPREAD, dev(wrap(z + i), wrap(y + j), k, x)), first_chip)

    pl.when(jnp.logical_not(owns))(remote(prow, prow, ROWS, ROWS, sibling).wait_recv)
    both = stack(split(prow[...]))

    def multiply(kk, i):
        new = dot16(both, a_hi[kk, i]) + dot16(both, a_lo[kk, i])
        return new[:NB] + new[NB:]

    for i in range(SIDE):
        new = multiply(1 - k, i)
        for q in range(SIDE):
            dbuf[1 - k, i, q] = new[:, q * 128 : (q + 1) * 128]
        launch(remote(dbuf.at[1 - k, i], sbuf.at[i], HALVES + i, HALVES + i, sibling))

    for i in range(SIDE):
        j = wrap(y + i)
        new = multiply(k, j)
        came(sbuf.at[j], HALVES + j)
        for q in range(SIDE):
            dbuf[k, j, q] = new[:, q * 128 : (q + 1) * 128] + sbuf[j, q]
        for h in (2, 1, 3, 0):
            if h or i:
                q = wrap(z + h)
                slot = SCATTER + 4 * h + i
                launch(remote(dbuf.at[k, j, q], rbuf.at[4 * h + i], slot, slot, dev(q, j, k, x)))

    pl.when(jnp.logical_not(first_chip))(gt_came)
    factors = []
    for _ in factor(gt_ref[...], r_ref, u_ref, factors):
        pass
    m_all, t_all = factors
    mt = jnp.transpose(stack([m_all, jnp.zeros_like(m_all)]))[:NB, :NB]
    r_all = r_ref[...]
    r_shift = jnp.transpose(r_all)[:NB, :]
    l_inv = t_all[:, NB:]
    k_t = -dot(l_inv, r_all[NB:, NB:])

    pl.when(self_home)(home_local.wait)
    pl.when(jnp.logical_not(self_home))(remote(pq, pq, HOME, HOME, sibling).wait_recv)
    piece = pq[0:NB] - jnp.where(first_row & owns, r_shift, 0.0)
    early = stack([dot(l_inv, pq[NB : 2 * NB]), dot(mt, piece)])
    total = dbuf[k, y, z]
    for slot in range(1, 16):
        came(rbuf.at[slot], SCATTER + slot)
        total = total + rbuf[slot]
    wv[k, y, z] = early + stack([dot(k_t, total), jnp.zeros_like(total)])

    for i, j in AROUND:
        slot = GATHER + 4 * i + j
        launch(remote(wv.at[k, y, z], wv.at[k, y, z], slot, slot, dev(wrap(z + i), wrap(y + j), k, x)))

    diagonal = x == z
    rows_local = pltpu.make_async_copy(wv.at[k, y, z], wv_rows.at[z], load_sem.at[8])

    def rows_copy(d):
        return remote(wv.at[k, y, z], wv_rows.at[z], OWN_ROWS + d, OWN_ROWS + z, dev(x, y, k, wrap(x + d)))

    pl.when(diagonal)(rows_local.start)
    launch(rows_copy(0), jnp.logical_not(diagonal))
    for d in (2, 1, 3):
        launch(rows_copy(d))
    b_t = dot(k_t, u_ref[:, :NB], NT)

    def gathered(j):
        for i in (0, 1, 3, 2):
            if i or j:
                came(wv.at[k, wrap(y + SIDE - j), wrap(z + SIDE - i)], GATHER + i * SIDE + j)
        there = wv.at[k, wrap(y + SIDE - j)]
        launch(remote(there, there, GATHER + 16 + j, GATHER + 16 + j, sibling))

    def sibling_came(j):
        came(wv.at[1 - k, wrap(y + SIDE - j)], GATHER + 16 + j)

    corner = [jnp.zeros((2 * NB, 2 * NB), jnp.float32)]

    def use(kk, i):
        hi, lo = split(jnp.concatenate([wv[kk, i, q] for q in range(SIDE)], axis=1))
        z_out[:, pl.ds(pl.multiple_of(i * 1024 + kk * 512, 512), 512)] = stack([hi, hi, lo])
        corner[0] = corner[0] + dot16(stack([hi[NB:], lo[NB:]]), stack([hi[:NB], lo[:NB]]), NT)

    for j in (0, 1, 3, 2):
        gathered(j)
        use(k, wrap(y + SIDE - j))
    for j in (0, 1, 3, 2):
        sibling_came(j)
        use(1 - k, wrap(y + SIDE - j))
    corner = corner[0][:NB] + corner[0][NB:]
    cbuf[x] = corner
    exchange(cbuf, CORNER)

    for d in range(1, SIDE):
        q = wrap(z + d)
        came(wv_rows.at[q], OWN_ROWS + q)
    pl.when(diagonal)(rows_local.wait)
    pl.when(jnp.logical_not(diagonal))(remote(wv_rows.at[z], wv_rows.at[z], OWN_ROWS, OWN_ROWS + z, sibling).wait_recv)
    own = jnp.concatenate([wv_rows[q] for q in range(SIDE)], axis=1)
    w_t, v_t = own[:NB], own[NB:]
    vt_out[...] = v_t
    finish()
    total = exchanged(cbuf, CORNER)
    w_t = w_t - dot(b_t, dot(total[:, :NB] + total[:, NB:], v_t))
    x_hi, x_lo = split(jnp.transpose(stack([v_t, w_t])))
    x_out[...] = jnp.concatenate([x_hi, x_lo, x_hi], axis=1)
    finish()


def update_kernel(a_ref, x_ref, z_ref, v_ref, out_ref, v_out):
    width = out_ref.shape[1]
    cols = pl.ds(pl.multiple_of(pl.program_id(0) * width, width), width)
    out_ref[...] = a_ref[:, cols] - dot16(x_ref[...], z_ref[:, cols])
    v_out[...] = v_ref[...]


def local(trailing):
    rows, cols = trailing.shape
    f32, b16 = jnp.float32, jnp.bfloat16
    vmem = pl.BlockSpec(memory_space=pltpu.VMEM)
    a_copy, x_mat, z_mat, v_t = pl.pallas_call(
        kernel,
        out_shape=(
            jax.ShapeDtypeStruct((rows, cols), f32),
            jax.ShapeDtypeStruct((rows, 6 * NB), b16),
            jax.ShapeDtypeStruct((6 * NB, cols), b16),
            jax.ShapeDtypeStruct((NB, rows), f32),
        ),
        in_specs=[pl.BlockSpec(memory_space=pl.ANY)],
        out_specs=(vmem, vmem, vmem, vmem),
        scratch_shapes=[
            pltpu.VMEM((2, SIDE, rows, 512), b16),
            pltpu.VMEM((2, SIDE, rows, 512), b16),
            pltpu.VMEM((rows, 128), f32),
            pltpu.VMEM((NB, cols), f32),
            pltpu.VMEM((SIDE, 128, 128), f32),
            pltpu.VMEM((NB, rows), f32),
            pltpu.VMEM((128, 128), f32),
            pltpu.VMEM((2, SIDE, SIDE, NB, 128), f32),
            pltpu.VMEM((SIDE, SIDE, NB, 128), f32),
            pltpu.VMEM((SIDE * SIDE, NB, 128), f32),
            pltpu.VMEM((2, SIDE, SIDE, 128, 128), f32),
            pltpu.VMEM((SIDE, 128, 128), f32),
            pltpu.VMEM((SIDE, NB, 128), f32),
            pltpu.VMEM((NB, 128), f32),
            pltpu.VMEM((SIDE, NB, 128), f32),
            pltpu.VMEM((128, 128), f32),
            pltpu.VMEM((NB, 128), f32),
            pltpu.SemaphoreType.DMA((9,)),
            pltpu.SemaphoreType.DMA((COUNT,)),
            pltpu.SemaphoreType.DMA((COUNT,)),
        ],
        compiler_params=pltpu.CompilerParams(
            collective_id=0, has_side_effects=True, vmem_limit_bytes=38 * 2**20
        ),
    )(trailing)
    step = 512
    reduced, v_t = pl.pallas_call(
        update_kernel,
        grid=(cols // step,),
        out_shape=(jax.ShapeDtypeStruct((rows, cols), f32), jax.ShapeDtypeStruct((NB, rows), f32)),
        in_specs=[vmem, vmem, vmem, vmem],
        out_specs=(pl.BlockSpec((rows, step), lambda i: (0, i)), pl.BlockSpec((NB, rows), lambda i: (0, 0))),
        compiler_params=pltpu.CompilerParams(vmem_limit_bytes=20 * 2**20),
    )(a_copy, x_mat, z_mat, v_t)
    return reduced, v_t.T


def solution(mesh):
    return jax.shard_map(
        local, mesh=mesh, in_specs=(P("row", "col"),), out_specs=(P("row", "col"), P("row", None)), check_vma=False
    )
```

time: 829 us -> 61.8 us (0.07)
  loops' own time: 216 us -> 0 us
  waiting for transfers between devices: 175 us -> 0 us
  blocking collectives: 139 us -> 0 us
  local copies, waits for them, and re-layouts: 122 us -> 0 us
  matrix products: 113 us -> 0 us
  Pallas kernels: 0 us -> 61 us
  other arithmetic: 43.2 us -> 0 us
  between operations: 14 us -> 0.64 us
    another operation x2 -> x0, loops' own time: 216 us -> none  [the longest x1 174 us: local(): lax.fori_loop(0, NB, body_turn, start + (top_rows,))]
    psum x2 -> x0, blocking collectives: 139 us -> none  [the longest x1 126 us: local(): panel_gram, top_rows = lax.psum((local_gram, local_top), 'row')]
    dynamic_slice x192 -> x0, local copies, waits for them, and re-layouts: 120 us -> none  [the longest x64 41.7 us: reflect_column(): leading = pivot_row[step_col]]
    dot_general x141 -> x0, matrix products: 113 us -> none  [the longest x64 50.3 us: block_turn(): column = -factor * jnp.dot(block, prior, precision=highest)]
    all_gather x2 -> x0, waiting for transfers between devices: 96.4 us -> none  [the longest x1 51.9 us: local(): every_row = lax.all_gather(vectors, 'row', axis=0, tiled=True)]
    psum x2 -> x0, waiting for transfers between devices: 78.2 us -> none  [the longest x1 40.4 us: from_root(): return lax.psum(jnp.where(mine, array, jnp.zeros_like(array)), axis)]
    pallas_call x0 -> x2, Pallas kernels: none -> 61 us  [the longest x1 54.9 us: local(): pl.pallas_call(kernel, out_shape=(jax.ShapeDtypeStruct((rows, cols), f32)...]
    select_n x323 -> x0, other arithmetic: 26.6 us -> none  [the longest x128 11 us: reflect_column(): jnp.where((columns == step_col)[None, :], new_column[:, None], panel_cols)]
  transfers between devices with their start and end apart: 4 -> 0, of which waited for: 4 -> 0; matrix products, arithmetic and copies ran while one was open for 1% -> 0% of each run, Pallas kernels for 0% -> 0%
where the time goes in v2:
time: 61.8 us; the launch traced here: 61.6 us
  Pallas kernels  61 us (99%)
  between operations  0.64 us (1%)
    pallas_call x1, Pallas kernels, local(): pl.pallas_call(kernel, out_shape=(jax.ShapeDtypeStruct((rows, cols), f32)...  54.9 us
    pallas_call x1, Pallas kernels, local(): pl.pallas_call(update_kernel, grid=(cols // step,), out_shape=(jax.ShapeD...  6.1 us

profile of v2, /device:TPU:1, one launch (start us, length us, event | category | flops | bytes accessed | tf_op | source)
XLA Modules:
  0.0 61.6 jit_solution(959417023105036291)
XLA Ops:
  0.6 54.9 %shard_map.30 = (f32[512,4096]{1,0:T(8,128)S(1)}, bf16[512,384]{1,0:T(8,128)(2,1)S(1)}, bf16[384,4096]{1,0:T(8,128)(2,1)S(1)}, f32[64,512]{1,0:T(8,128)S(1)}) custom-call(f32[512,4096]{1,0:T(8,128)} %a_hbm.1), custom_call_target="tpu_custom_call" | custom-call | tf_op jit(solution)/shard_map/pallas_call | solution.py:379
  55.5 6.1 %shard_map.31 = (f32[512,4096]{1,0:T(8,128)}, f32[64,512]{1,0:T(8,128)}) custom-call(f32[512,4096]{1,0:T(8,128)S(1)} %get-tuple-element.8.a_ref, bf16[512,384]{1,0:T(8,128)(2,1)S(1)} %get-tuple-element.9.x_ref, bf16[384,4096]{1,0:T(8,128)(2,1)S(1)} %get-tuple-element.10.z_ref, f32[64,512]{1,0:T(8,128)S(1)} %get-tuple-element.11.v_ref), custom_call_target="tpu_custom_call" | custom-call | tf_op jit(solution)/shard_map/pallas_call | solution.py:416

commit v3 on v2

v3 whole, which is shorter than its diff:
```python
import jax
import jax.numpy as jnp
from jax import lax
from jax.experimental import pallas as pl
from jax.experimental.pallas import tpu as pltpu
from jax.sharding import PartitionSpec as P

NB = 64
BLOCK = 8
SIDE = 4
MESH = pl.DeviceIdType.MESH
HIGHEST = lax.Precision.HIGHEST
NN = (((1,), (0,)), ((), ()))
NT = (((1,), (1,)), ((), ()))
TN = (((0,), (0,)), ((), ()))


def dot(a, b, dims=NN):
    return lax.dot_general(a, b, dims, precision=HIGHEST, preferred_element_type=jnp.float32)


def dot16(a, b, dims=NN):
    return lax.dot_general(a, b, dims, preferred_element_type=jnp.float32)


def split(a):
    high = a.astype(jnp.bfloat16)
    return high, (a - high.astype(jnp.float32)).astype(jnp.bfloat16)


def split3(a):
    high = a.astype(jnp.bfloat16)
    rest = a - high.astype(jnp.float32)
    middle = rest.astype(jnp.bfloat16)
    return high, middle, (rest - middle.astype(jnp.float32)).astype(jnp.bfloat16)


def stack(parts):
    return jnp.concatenate(parts, axis=0)


def wrap(i):
    return i & (SIDE - 1)


def wrap_core(i):
    return i & 1


AROUND = [(2, 2), (2, 1), (2, 3), (1, 2), (3, 2), (1, 1), (3, 3), (1, 3), (3, 1), (2, 0), (0, 2), (1, 0), (3, 0), (0, 1), (0, 3)]


RING = (2, 1, 3, 0)


class Ids:
    def __init__(self):
        self.count = 0

    def take(self, n):
        first = self.count
        self.count += n
        return first


IDS = Ids()
ROWS = IDS.take(4)
HOME_P = IDS.take(32)
HOME_Q = IDS.take(4)
GRAM = IDS.take(8)
SPREAD = IDS.take(17)
HALVES = IDS.take(4)
SCATTER = IDS.take(16)
GATHER_P = IDS.take(10)
GATHER_W = IDS.take(20)
OWN_ROWS = IDS.take(4)
CORNER = IDS.take(8)
COUNT = IDS.count


def factor(gt, r_ref, c_ref, l_ref):
    lanes = lax.broadcasted_iota(jnp.int32, (8, 128), 1)
    subs = lax.broadcasted_iota(jnp.int32, (8, 128), 0)
    lane = lax.broadcasted_iota(jnp.int32, (1, 128), 1)
    t_all = jnp.transpose(stack([gt, jnp.zeros_like(gt)]))[NB:, :]
    S, T = [], []
    for b in range(8):
        rows = slice(8 * b, 8 * b + 8)
        unit = jnp.where(lanes == subs + (8 * b + NB), 1.0, 0.0)
        S.append(jnp.where(lanes < NB, gt[rows], unit))
        T.append(jnp.where(lanes < NB, t_all[rows], unit))

    def spread(row, j):
        return jnp.broadcast_to(row[:, j : j + 1], (1, 128))

    for j0 in range(0, NB, BLOCK):
        b, s0 = j0 // 8, j0 % 8
        srow = [S[b][s0 + p : s0 + p + 1, :] for p in range(BLOCK)]
        trow = [T[b][s0 + p : s0 + p + 1, :] for p in range(BLOCK)]
        s = [[spread(srow[p], j0 + q) if q >= p else None for q in range(BLOCK)] for p in range(BLOCK)]
        t = [[spread(trow[p], j0 + q) for q in range(BLOCK)] for p in range(BLOCK)]
        d_inv, root_inv, length, f = [], [], [], {}
        for p in range(BLOCK):
            d_inv.append(1.0 / s[p][p])
            root_inv.append(lax.rsqrt(s[p][p]))
            length.append(s[p][p] * root_inv[p])
            for i in range(p + 1, BLOCK):
                f[p, i] = s[p][i] * d_inv[p]
                for q in range(i, BLOCK):
                    s[i][q] = s[i][q] - f[p, i] * s[p][q]
                srow[i] = srow[i] - f[p, i] * srow[p]
        surow = [srow[p] * d_inv[p] for p in range(BLOCK)]
        turow, g = [], {}
        for p in range(BLOCK):
            j = j0 + p
            positive = t[p][p] >= 0.0
            pivot_inv = 1.0 / (jnp.abs(t[p][p]) + length[p])
            pivot_inv = jnp.where(positive, pivot_inv, -pivot_inv)
            lead_inv = jnp.where(positive, -root_inv[p], root_inv[p])
            rrow = jnp.where(lane >= j, srow[p] * lead_inv, 0.0)
            r_ref[NB + j : NB + j + 1, :] = rrow
            urow = jnp.where(lane < NB, trow[p] - rrow, trow[p])
            l_ref[j : j + 1, :] = trow[p]
            turow.append(urow * pivot_inv)
            later = jnp.where(lane == j, 1.0 - pivot_inv, turow[p])
            c_ref[j : j + 1, :] = jnp.where((lane >= j) & (lane < NB), later, 0.0)
            for q in range(p + 1, BLOCK):
                g[p, q] = (t[p][q] - s[p][q] * lead_inv) * pivot_inv
            for i in range(p + 1, BLOCK):
                for q in range(p + 1, BLOCK):
                    t[i][q] = t[i][q] - t[i][p] * g[p, q]
                trow[i] = trow[i] - t[i][p] * turow[p]
        for m in range((j0 + BLOCK) // 8, 8):
            sc, tc = [], []
            for p in range(BLOCK):
                sp, tp = S[m][:, j0 + p : j0 + p + 1], T[m][:, j0 + p : j0 + p + 1]
                sp, tp = jnp.broadcast_to(sp, (8, 128)), jnp.broadcast_to(tp, (8, 128))
                for i in range(p):
                    sp = sp - sc[i] * f[i, p]
                    tp = tp - tc[i] * g[i, p]
                sc.append(sp)
                tc.append(tp)
            for p in range(BLOCK):
                S[m] = S[m] - sc[p] * surow[p]
                T[m] = T[m] - tc[p] * turow[p]


def invert(c_ref):
    lanes = lax.broadcasted_iota(jnp.int32, (8, 128), 1)
    subs = lax.broadcasted_iota(jnp.int32, (8, 128), 0)
    C = [jnp.where(lanes == subs + 8 * b, 1.0, 0.0) for b in range(8)]
    for j0 in range(0, NB, BLOCK):
        rows = [c_ref[j0 + p : j0 + p + 1, :] for p in range(BLOCK)]
        g = {(i, p): jnp.broadcast_to(rows[i][:, j0 + p : j0 + p + 1], (1, 128)) for p in range(BLOCK) for i in range(p)}
        for m in range(j0 // 8 + 1):
            cols = []
            for p in range(BLOCK):
                col = jnp.broadcast_to(C[m][:, j0 + p : j0 + p + 1], (8, 128))
                for i in range(p):
                    col = col - cols[i] * g[i, p]
                cols.append(col)
            for p in range(BLOCK):
                C[m] = C[m] - cols[p] * rows[p]
    return stack(C)


def kernel(
    a_hbm, a_v, x_out, z_out, vt_out,
    a_hi, a_lo, head, lead, panel, prow, qpiece, dbuf, sbuf, rbuf, pbuf, wbuf, wrow, gbuf, gt_ref, cbuf, r_ref, c_ref, l_ref,
    load_sem, send, recv,
):
    r, x = lax.axis_index("row"), lax.axis_index("col")
    z, y, k = r // 8, lax.rem(r // 2, SIDE), lax.rem(r, 2)
    w = (1 - k) * z + k * y
    u = (1 - k) * y + k * z
    lanes64 = lax.broadcasted_iota(jnp.int32, (NB, 128), 1)

    def dev(z_, y_, k_, x_):
        return (z_ * 8 + y_ * 2 + k_, x_)

    def dev_w(d):
        return dev(wrap(z + d * (1 - k)), wrap(y + d * k), k, x)

    def dev_u(d):
        return dev(wrap(z + d * k), wrap(y + d * (1 - k)), k, x)

    def remote(src, dst, s, t, device):
        return pltpu.make_async_remote_copy(
            src_ref=src, dst_ref=dst, send_sem=send.at[s], recv_sem=recv.at[t],
            device_id=device, device_id_type=MESH,
        )

    sends = []

    def launch(copy, when=None):
        if when is None:
            copy.start()
        else:
            pl.when(when)(copy.start)
        sends.append((copy, when))

    def finish():
        for copy, when in sends:
            if when is None:
                copy.wait_send()
            else:
                pl.when(when)(copy.wait_send)
        sends.clear()

    sibling = dev(z, y, 1 - k, x)

    def came(dst, slot):
        remote(dst, dst, slot, slot, sibling).wait_recv()

    owns = x == 0
    first_row = r == 0
    first_chip = r < 2
    half = a_v.shape[0] // 2

    def head_load(q):
        rows = pl.ds(q * 128, 128)
        return pltpu.make_async_copy(a_hbm.at[rows, pl.ds(0, 128)], head.at[rows], load_sem.at[q])

    def load(i):
        rows = pl.ds(i * half, half)
        return pltpu.make_async_copy(a_hbm.at[rows], a_v.at[rows], load_sem.at[4 + i])

    lead_load = pltpu.make_async_copy(a_hbm.at[pl.ds(0, NB)], lead, load_sem.at[6])

    @pl.when(owns)
    def _():
        for q in range(SIDE):
            head_load(q).start()

    pl.when(first_row)(lead_load.start)
    barrier = pltpu.get_barrier_semaphore()
    peers = [dev(wrap(z + i), y, k, wrap(x + j)) for i in range(SIDE) for j in range(1, SIDE)]
    peers += [dev(wrap(z + i), wrap(y + j), k, x) for i, j in AROUND] + [sibling]
    peers += [dev(z, y, 1 - k, wrap(x + j)) for j in range(1, SIDE)]
    for peer in peers:
        pl.semaphore_signal(barrier, inc=1, device_id=peer, device_id_type=MESH)

    @pl.when((k == 1) & (r != 1))
    def _():
        pl.semaphore_signal(barrier, inc=1, device_id=dev(0, 0, 0, x), device_id_type=MESH)

    load(0).start()
    load(1).start()
    r_ref[0:NB, :] = jnp.zeros((NB, 128), jnp.float32)

    @pl.when(owns)
    def _():
        for q in range(SIDE):
            head_load(q).wait()
            panel[q] = jnp.transpose(head[q * 128 : (q + 1) * 128, :])
            if q == 0:
                panel[0, 0:NB] = jnp.where(first_row & (lanes64 < NB), 0.0, panel[0, 0:NB])
            prow[:, q * 128 : (q + 1) * 128] = panel[q, 0:NB]

    @pl.when(first_row)
    def _():
        lead_load.wait()
        lead[:, 0:128] = jnp.where(owns & (lanes64 < NB), 0.0, lead[:, 0:128])
        gram = jnp.zeros((3 * NB, 3 * NB), jnp.float32)
        for m in range(8):
            three = stack(split3(lead[:, m * 512 : (m + 1) * 512]))
            gram = gram + dot16(three, three, NT)
        gram = gram[:NB] + gram[NB : 2 * NB] + gram[2 * NB :]
        gram = gram[:, :NB] + gram[:, NB : 2 * NB] + gram[:, 2 * NB :]
        top = jnp.where(owns, lead[:, 0:128], 0.0)
        gbuf[x] = jnp.where(lanes64 < NB, jnp.concatenate([gram, gram], axis=1), top)

    def split_rows(part_id):
        load(part_id).wait()

        def body(step, carry):
            rows = pl.ds(pl.multiple_of(part_id * half + step * 16, 16), 16)
            for kk in range(2):
                for i in range(SIDE):
                    first = i * 1024 + kk * 512
                    a_hi[kk, i, rows, :], a_lo[kk, i, rows, :] = split(a_v[rows, first : first + 512])
            return carry

        lax.fori_loop(0, half // 16, body, 0)

    @pl.when(first_chip)
    def _():
        split_rows(0)
        split_rows(1)

    @pl.when(first_row)
    def _():
        pl.semaphore_wait(barrier, len(peers) + SIDE * SIDE - 1)

    @pl.when(jnp.logical_not(first_row))
    def _():
        pl.semaphore_wait(barrier, len(peers))


    for d in (2, 1, 3):
        launch(remote(prow, prow, ROWS + d, ROWS, dev(z, y, k, d)), owns)
    diagonal = x == z
    off_diagonal = jnp.logical_not(diagonal)

    def home_q(q):
        return remote(panel.at[q, pl.ds(NB, NB)], qpiece, HOME_Q + q, HOME_Q, dev(q, y, k, z))

    self_home = owns & (z == 0)
    home_local = pltpu.make_async_copy(panel.at[0, pl.ds(NB, NB)], qpiece, load_sem.at[7])

    def exchanged(buf, base):
        for d in range(1, SIDE):
            came(buf.at[wrap(x + SIDE - d)], base + d)
        return (buf[0] + buf[1]) + (buf[2] + buf[3])

    def own_piece():
        pbuf[0, 0, 0] = lead[:, 0:128]

    for d in (2, 1, 3):
        for kk in range(2):
            slot = GRAM + 2 * d + kk
            launch(remote(gbuf.at[x], gbuf.at[x], slot, GRAM + d, dev(0, 0, kk, wrap(x + d))), first_row)
    launch(remote(gbuf.at[x], gbuf.at[x], GRAM, GRAM, sibling), first_row)

    pl.when(first_row)(own_piece)
    for i, j in AROUND + [(0, 0)]:
        for kk in range(2):
            if i or j or kk:
                there = pbuf.at[kk, i if kk else j, j if kk else i]
                piece = lead.at[:, pl.ds(j * 1024 + kk * 512 + i * 128, 128)]
                launch(remote(piece, there, HOME_P + kk * 16 + i * SIDE + j, HOME_P, dev(i, j, kk, x)), first_row)

    @pl.when(jnp.logical_not(first_chip))
    def _():
        split_rows(0)
        split_rows(1)

    pl.when(r == 1)(remote(gbuf.at[x], gbuf.at[x], GRAM, GRAM, sibling).wait_recv)

    @pl.when(first_chip)
    def _():
        gt_ref[...] = exchanged(gbuf, GRAM)

    def gt_came():
        came(gt_ref, SPREAD)

    for i, j in AROUND:
        launch(remote(gt_ref, gt_ref, SPREAD + 4 * i + j, SPREAD, dev(wrap(z + i), wrap(y + j), k, x)), first_chip)

    pl.when(jnp.logical_not(owns))(remote(prow, prow, ROWS, ROWS, sibling).wait_recv)
    both = stack(split(prow[...]))

    def multiply(kk, i):
        new = dot16(both, a_hi[kk, i]) + dot16(both, a_lo[kk, i])
        return new[:NB] + new[NB:]

    for i in RING:
        j = wrap(y + i)
        new = multiply(1 - k, j)
        for q in range(SIDE):
            dbuf[1 - k, j, q] = new[:, q * 128 : (q + 1) * 128]
        launch(remote(dbuf.at[1 - k, j], sbuf.at[j], HALVES + i, HALVES + i, sibling))

    pl.when(jnp.logical_not(first_row))(remote(pbuf.at[k, u, w], pbuf.at[k, u, w], HOME_P, HOME_P, sibling).wait_recv)
    for d in (2, 1, 3):
        launch(remote(pbuf.at[k, u, w], pbuf.at[k, u, w], GATHER_P + d - 1, GATHER_P + d - 1, dev_w(d)))

    for i in RING:
        j = wrap(y + i)
        new = multiply(k, j)
        came(sbuf.at[j], HALVES + i)
        for q in range(SIDE):
            dbuf[k, j, q] = new[:, q * 128 : (q + 1) * 128] + sbuf[j, q]
        for h in RING:
            if h or i:
                q = wrap(z + h)
                slot = SCATTER + 4 * h + i
                launch(remote(dbuf.at[k, j, q], rbuf.at[4 * h + i], slot, slot, dev(q, j, k, x)))

    pl.when(self_home)(home_local.start)
    launch(home_q(0), owns & (z != 0))
    for q in range(1, SIDE):
        launch(home_q(q), owns)

    def sibling_send(buf, i, slot):
        launch(remote(buf.at[k, i], buf.at[k, i], slot, slot, sibling))

    for d in (1, 3, 2):
        came(pbuf.at[k, u, wrap(w + SIDE - d)], GATHER_P + d - 1)
    for d in (2, 1, 3):
        launch(remote(pbuf.at[k, u], pbuf.at[k, u], GATHER_P + 2 + d, GATHER_P + 2 + d, dev_u(d)))
    pl.when(jnp.logical_not(first_chip))(gt_came)
    factor(gt_ref[...], r_ref, c_ref, l_ref)
    r_all = r_ref[...]
    r_shift = jnp.transpose(r_all)[:NB, :]
    l_inv = l_ref[:, NB:]
    k_t = -dot(l_inv, r_all[NB:, NB:])

    pl.when(self_home)(home_local.wait)
    pl.when(jnp.logical_not(self_home))(remote(qpiece, qpiece, HOME_Q, HOME_Q, sibling).wait_recv)
    early = dot(l_inv, qpiece[...])
    total = dbuf[k, y, z]
    for slot in range(1, 16):
        came(rbuf.at[slot], SCATTER + slot)
        total = total + rbuf[slot]
    w_piece = early + dot(k_t, total)
    p_piece = pbuf[k, u, w] - jnp.where(first_row & owns, r_shift, 0.0)
    corner = dot(k_t, dot(p_piece, w_piece, NT))
    wbuf[k, y, z, 0:NB] = w_piece
    wbuf[k, y, z, NB:] = jnp.concatenate([corner[: NB // 2], corner[NB // 2 :]], axis=1)
    for i, j in AROUND:
        slot = GATHER_W + 4 * i + j
        launch(remote(wbuf.at[k, y, z], wbuf.at[k, y, z], slot, slot, dev(wrap(z + i), wrap(y + j), k, x)))
    rows_local = pltpu.make_async_copy(wbuf.at[k, y, z, pl.ds(0, NB)], wrow.at[z], load_sem.at[8])

    def rows_copy(d):
        return remote(wbuf.at[k, y, z, pl.ds(0, NB)], wrow.at[z], OWN_ROWS + d, OWN_ROWS + z, dev(x, y, k, wrap(x + d)))

    pl.when(diagonal)(rows_local.start)
    launch(rows_copy(0), off_diagonal)
    for d in (2, 1, 3):
        launch(rows_copy(d))

    m_all = invert(c_ref)
    mt = jnp.transpose(stack([m_all, jnp.zeros_like(m_all)]))[:NB, :NB]
    mt_hi, mt_lo = split(mt)
    shift = jnp.where(first_row, r_shift, 0.0)
    v_t = dot(mt, jnp.concatenate([prow[:, :128] - shift, prow[:, 128:]], axis=1))
    vt_out[...] = v_t
    shift = jnp.where(owns, r_shift, 0.0)

    def put(row, cols, hi, lo):
        z_out[row : row + NB, cols] = hi
        z_out[row + 2 * NB : row + 3 * NB, cols] = hi
        z_out[row + 4 * NB : row + 5 * NB, cols] = lo

    def make_v(kk, i):
        piece = jnp.concatenate([pbuf[kk, i, j] for j in range(SIDE)], axis=1)
        lead_shift = jnp.where((kk == 0) & (i == 0), shift, 0.0)
        hi, lo = split(jnp.concatenate([piece[:, :128] - lead_shift, piece[:, 128:]], axis=1))
        hi, lo = split((dot16(mt_lo, hi) + dot16(mt_hi, lo)) + dot16(mt_hi, hi))
        for j in range(SIDE):
            first = (1 - kk) * (i * 1024 + j * 128) + kk * (j * 1024 + 512 + i * 128)
            here = slice(j * 128, (j + 1) * 128)
            put(NB, pl.ds(pl.multiple_of(first, 128), 128), hi[:, here], lo[:, here])

    sibling_send(pbuf, u, GATHER_P + 6)
    for d in (1, 3, 2):
        came(pbuf.at[k, wrap(u + SIDE - d)], GATHER_P + 2 + d)
        sibling_send(pbuf, wrap(u + SIDE - d), GATHER_P + 6 + d)
    for d in range(SIDE):
        make_v(k, wrap(u + SIDE - d))
    for d in range(SIDE):
        came(pbuf.at[1 - k, wrap(w + SIDE - d)], GATHER_P + 6 + d)
        make_v(1 - k, wrap(w + SIDE - d))

    def use_w(kk, i):
        hi, lo = split(jnp.concatenate([wbuf[kk, i, q, 0:NB] for q in range(SIDE)], axis=1))
        put(0, pl.ds(pl.multiple_of(i * 1024 + kk * 512, 512), 512), hi, lo)

    corner = jnp.zeros((NB // 2, 128), jnp.float32)
    for j in (0, 1, 3, 2):
        for i in (0, 1, 3, 2):
            if i or j:
                came(wbuf.at[k, wrap(y + SIDE - j), wrap(z + SIDE - i)], GATHER_W + i * SIDE + j)
        sibling_send(wbuf, wrap(y + SIDE - j), GATHER_W + 16 + j)
    for i in range(SIDE):
        for q in range(SIDE):
            corner = corner + wbuf[k, i, q, NB:]
    cbuf[4 * k + x] = corner
    for d in (2, 1, 3):
        for kk in range(2):
            slot = CORNER + 2 * d + kk
            there = cbuf.at[4 * k + x]
            launch(remote(there, there, slot, slot, dev(z, y, wrap_core(k + kk), wrap(x + d))))
    launch(remote(cbuf.at[4 * k + x], cbuf.at[4 * k + x], CORNER + 1, CORNER + 1, sibling))

    for j in RING:
        use_w(k, wrap(y + SIDE - j))
    for j in (0, 1, 3, 2):
        came(wbuf.at[1 - k, wrap(y + SIDE - j)], GATHER_W + 16 + j)
        use_w(1 - k, wrap(y + SIDE - j))

    def own_came():
        for d in range(1, SIDE):
            q = wrap(z + d)
            came(wrow.at[q], OWN_ROWS + q)
        pl.when(diagonal)(rows_local.wait)
        pl.when(off_diagonal)(remote(wrow.at[z], wrow.at[z], OWN_ROWS, OWN_ROWS + z, sibling).wait_recv)

    own_came()
    w_t = jnp.concatenate([wrow[q] for q in range(SIDE)], axis=1)
    finish()
    came(cbuf.at[4 * wrap_core(k + 1) + x], CORNER + 1)
    for d in range(1, SIDE):
        for kk in range(2):
            came(cbuf.at[4 * wrap_core(k + kk) + wrap(x + SIDE - d)], CORNER + 2 * d + kk)
    corner = cbuf[0]
    for i in range(1, 2 * SIDE):
        corner = corner + cbuf[i]
    w_t = w_t - dot(stack([corner[:, :NB], corner[:, NB:]]), v_t)
    x_hi, x_lo = split(jnp.transpose(stack([v_t, w_t])))
    x_out[...] = jnp.concatenate([x_hi, x_lo, x_hi], axis=1)
    finish()


def update_kernel(a_ref, x_ref, z_ref, v_ref, out_hbm, v_hbm, buf, sem):
    parts, _, width = buf.shape
    v_copy = pltpu.make_async_copy(v_ref, v_hbm, sem.at[parts])
    v_copy.start()
    copies = []
    for i in range(parts):
        cols = slice(i * width, (i + 1) * width)
        buf[i] = a_ref[:, cols] - dot16(x_ref[...], z_ref[:, cols])
        copies.append(pltpu.make_async_copy(buf.at[i], out_hbm.at[:, pl.ds(i * width, width)], sem.at[i]))
        copies[i].start()
    for copy in copies:
        copy.wait()
    v_copy.wait()


def local(trailing):
    rows, cols = trailing.shape
    f32, b16 = jnp.float32, jnp.bfloat16
    vmem = pl.BlockSpec(memory_space=pltpu.VMEM)
    pieces = pltpu.VMEM((2, SIDE, SIDE, NB, 128), f32)
    square = pltpu.VMEM((SIDE, NB, 128), f32)
    a_copy, x_mat, z_mat, v_t = pl.pallas_call(
        kernel,
        out_shape=(
            jax.ShapeDtypeStruct((rows, cols), f32),
            jax.ShapeDtypeStruct((rows, 6 * NB), b16),
            jax.ShapeDtypeStruct((6 * NB, cols), b16),
            jax.ShapeDtypeStruct((NB, rows), f32),
        ),
        in_specs=[pl.BlockSpec(memory_space=pl.ANY)],
        out_specs=(vmem, vmem, vmem, vmem),
        scratch_shapes=[
            pltpu.VMEM((2, SIDE, rows, 512), b16),
            pltpu.VMEM((2, SIDE, rows, 512), b16),
            pltpu.VMEM((rows, 128), f32),
            pltpu.VMEM((NB, cols), f32),
            pltpu.VMEM((SIDE, 128, 128), f32),
            pltpu.VMEM((NB, rows), f32),
            pltpu.VMEM((NB, 128), f32),
            pieces,
            pltpu.VMEM((SIDE, SIDE, NB, 128), f32),
            pltpu.VMEM((SIDE * SIDE, NB, 128), f32),
            pieces,
            pltpu.VMEM((2, SIDE, SIDE, NB + NB // 2, 128), f32),
            square,
            square,
            pltpu.VMEM((NB, 128), f32),
            pltpu.VMEM((2 * SIDE, NB // 2, 128), f32),
            pltpu.VMEM((128, 128), f32),
            pltpu.VMEM((NB, 128), f32),
            pltpu.VMEM((NB, 128), f32),
            pltpu.SemaphoreType.DMA((9,)),
            pltpu.SemaphoreType.DMA((COUNT,)),
            pltpu.SemaphoreType.DMA((COUNT,)),
        ],
        compiler_params=pltpu.CompilerParams(
            collective_id=0, has_side_effects=True, vmem_limit_bytes=38 * 2**20
        ),
    )(trailing)
    step = 512
    hbm = pl.BlockSpec(memory_space=pl.ANY)
    reduced, v_t = pl.pallas_call(
        update_kernel,
        out_shape=(jax.ShapeDtypeStruct((rows, cols), f32), jax.ShapeDtypeStruct((NB, rows), f32)),
        in_specs=[vmem, vmem, vmem, vmem],
        out_specs=(hbm, hbm),
        scratch_shapes=[pltpu.VMEM((cols // step, rows, step), f32), pltpu.SemaphoreType.DMA((cols // step + 1,))],
        compiler_params=pltpu.CompilerParams(vmem_limit_bytes=24 * 2**20),
    )(a_copy, x_mat, z_mat, v_t)
    return reduced, v_t.T


def solution(mesh):
    return jax.shard_map(
        local, mesh=mesh, in_specs=(P("row", "col"),), out_specs=(P("row", "col"), P("row", None)), check_vma=False
    )
```

time: 61.8 us -> 52.2 us (0.84)
  Pallas kernels: 61 us -> 51.4 us
    pallas_call x1, Pallas kernels: 54.9 us -> 47.6 us  [local(): pl.pallas_call(kernel, out_shape=(jax.ShapeDtypeStruct((rows, cols), f32)...]
    pallas_call x1, Pallas kernels: 6.1 us -> 3.82 us  [local(): pl.pallas_call(update_kernel, out_shape=(jax.ShapeDtypeStruct((rows, cols...]
where the time goes in v3:
time: 52.2 us; the launch traced here: 52.1 us
  Pallas kernels  51.4 us (98%)
  between operations  0.64 us (1%)
    pallas_call x1, Pallas kernels, local(): pl.pallas_call(kernel, out_shape=(jax.ShapeDtypeStruct((rows, cols), f32)...  47.6 us
    pallas_call x1, Pallas kernels, local(): pl.pallas_call(update_kernel, out_shape=(jax.ShapeDtypeStruct((rows, cols...  3.82 us

profile of v3, /device:TPU:1, one launch (start us, length us, event | category | flops | bytes accessed | tf_op | source)
XLA Modules:
  0.0 52.1 jit_solution(767950081424573364)
XLA Ops:
  0.6 47.6 %shard_map.30 = (f32[512,4096]{1,0:T(8,128)S(1)}, bf16[512,384]{1,0:T(8,128)(2,1)S(1)}, bf16[384,4096]{1,0:T(8,128)(2,1)S(1)}, f32[64,512]{1,0:T(8,128)S(1)}) custom-call(f32[512,4096]{1,0:T(8,128)} %a_hbm.1), custom_call_target="tpu_custom_call" | custom-call | tf_op jit(solution)/shard_map/pallas_call | solution.py:528
  48.2 3.8 %shard_map.31 = (f32[512,4096]{1,0:T(8,128)}, f32[64,512]{1,0:T(8,128)}) custom-call(f32[512,4096]{1,0:T(8,128)S(1)} %get-tuple-element.8.a_ref, bf16[512,384]{1,0:T(8,128)(2,1)S(1)} %get-tuple-element.9.x_ref, bf16[384,4096]{1,0:T(8,128)(2,1)S(1)} %get-tuple-element.10.z_ref, f32[64,512]{1,0:T(8,128)S(1)} %get-tuple-element.11.v_ref), custom_call_target="tpu_custom_call" | custom-call | tf_op jit(solution)/shard_map/pallas_call | solution.py:568

commit v4 on v3

--- a/solution.py
+++ b/solution.py
@@ -75,6 +75,7 @@
 GATHER_W = IDS.take(20)
 OWN_ROWS = IDS.take(4)
 CORNER = IDS.take(8)
+CORNER_P = IDS.take(16)
 COUNT = IDS.count
 
 
@@ -399,22 +400,29 @@
     pl.when(self_home)(home_local.wait)
     pl.when(jnp.logical_not(self_home))(remote(qpiece, qpiece, HOME_Q, HOME_Q, sibling).wait_recv)
     early = dot(l_inv, qpiece[...])
+    k_p = dot(k_t, pbuf[k, u, w] - jnp.where(first_row & owns, r_shift, 0.0))
     total = dbuf[k, y, z]
     for slot in range(1, 16):
         came(rbuf.at[slot], SCATTER + slot)
         total = total + rbuf[slot]
-    w_piece = early + dot(k_t, total)
-    p_piece = pbuf[k, u, w] - jnp.where(first_row & owns, r_shift, 0.0)
-    corner = dot(k_t, dot(p_piece, w_piece, NT))
-    wbuf[k, y, z, 0:NB] = w_piece
-    wbuf[k, y, z, NB:] = jnp.concatenate([corner[: NB // 2], corner[NB // 2 :]], axis=1)
+    wbuf[k, y, z] = early + dot(k_t, total)
+    corner = dot(k_p, wbuf[k, y, z], NT)
+    mine = 4 * k + x
+    cbuf[mine] = jnp.concatenate([corner[: NB // 2], corner[NB // 2 :]], axis=1)
+    for d in (2, 1, 3):
+        for kk in range(2):
+            slot = CORNER + 2 * d + kk
+            launch(remote(cbuf.at[mine], cbuf.at[mine], slot, slot, dev(z, y, wrap_core(k + kk), wrap(x + d))))
+    launch(remote(cbuf.at[mine], cbuf.at[mine], CORNER + 1, CORNER + 1, sibling))
+
     for i, j in AROUND:
         slot = GATHER_W + 4 * i + j
         launch(remote(wbuf.at[k, y, z], wbuf.at[k, y, z], slot, slot, dev(wrap(z + i), wrap(y + j), k, x)))
-    rows_local = pltpu.make_async_copy(wbuf.at[k, y, z, pl.ds(0, NB)], wrow.at[z], load_sem.at[8])
+
+    rows_local = pltpu.make_async_copy(wbuf.at[k, y, z], wrow.at[z], load_sem.at[8])
 
     def rows_copy(d):
-        return remote(wbuf.at[k, y, z, pl.ds(0, NB)], wrow.at[z], OWN_ROWS + d, OWN_ROWS + z, dev(x, y, k, wrap(x + d)))
+        return remote(wbuf.at[k, y, z], wrow.at[z], OWN_ROWS + d, OWN_ROWS + z, dev(x, y, k, wrap(x + d)))
 
     pl.when(diagonal)(rows_local.start)
     launch(rows_copy(0), off_diagonal)
@@ -422,6 +430,19 @@
         launch(rows_copy(d))
 
     m_all = invert(c_ref)
+
+    came(cbuf.at[4 * wrap_core(k + 1) + x], CORNER + 1)
+    for d in range(1, SIDE):
+        for kk in range(2):
+            came(cbuf.at[4 * wrap_core(k + kk) + wrap(x + SIDE - d)], CORNER + 2 * d + kk)
+    corner = cbuf[0]
+    for i in range(1, 8):
+        corner = corner + cbuf[i]
+    cbuf[8] = corner
+    for i, j in AROUND:
+        slot = 4 * i + j
+        launch(remote(cbuf.at[8], cbuf.at[8 + slot], CORNER_P + slot, CORNER_P + slot, dev(wrap(z + i), wrap(y + j), k, x)))
+
     mt = jnp.transpose(stack([m_all, jnp.zeros_like(m_all)]))[:NB, :NB]
     mt_hi, mt_lo = split(mt)
     shift = jnp.where(first_row, r_shift, 0.0)
@@ -455,26 +476,14 @@
         make_v(1 - k, wrap(w + SIDE - d))
 
     def use_w(kk, i):
-        hi, lo = split(jnp.concatenate([wbuf[kk, i, q, 0:NB] for q in range(SIDE)], axis=1))
+        hi, lo = split(jnp.concatenate([wbuf[kk, i, q] for q in range(SIDE)], axis=1))
         put(0, pl.ds(pl.multiple_of(i * 1024 + kk * 512, 512), 512), hi, lo)
 
-    corner = jnp.zeros((NB // 2, 128), jnp.float32)
     for j in (0, 1, 3, 2):
         for i in (0, 1, 3, 2):
             if i or j:
                 came(wbuf.at[k, wrap(y + SIDE - j), wrap(z + SIDE - i)], GATHER_W + i * SIDE + j)
         sibling_send(wbuf, wrap(y + SIDE - j), GATHER_W + 16 + j)
-    for i in range(SIDE):
-        for q in range(SIDE):
-            corner = corner + wbuf[k, i, q, NB:]
-    cbuf[4 * k + x] = corner
-    for d in (2, 1, 3):
-        for kk in range(2):
-            slot = CORNER + 2 * d + kk
-            there = cbuf.at[4 * k + x]
-            launch(remote(there, there, slot, slot, dev(z, y, wrap_core(k + kk), wrap(x + d))))
-    launch(remote(cbuf.at[4 * k + x], cbuf.at[4 * k + x], CORNER + 1, CORNER + 1, sibling))
-
     for j in RING:
         use_w(k, wrap(y + SIDE - j))
     for j in (0, 1, 3, 2):
@@ -491,13 +500,10 @@
     own_came()
     w_t = jnp.concatenate([wrow[q] for q in range(SIDE)], axis=1)
     finish()
-    came(cbuf.at[4 * wrap_core(k + 1) + x], CORNER + 1)
-    for d in range(1, SIDE):
-        for kk in range(2):
-            came(cbuf.at[4 * wrap_core(k + kk) + wrap(x + SIDE - d)], CORNER + 2 * d + kk)
-    corner = cbuf[0]
-    for i in range(1, 2 * SIDE):
-        corner = corner + cbuf[i]
+    corner = cbuf[8]
+    for slot in range(1, 16):
+        came(cbuf.at[8 + slot], CORNER_P + slot)
+        corner = corner + cbuf[8 + slot]
     w_t = w_t - dot(stack([corner[:, :NB], corner[:, NB:]]), v_t)
     x_hi, x_lo = split(jnp.transpose(stack([v_t, w_t])))
     x_out[...] = jnp.concatenate([x_hi, x_lo, x_hi], axis=1)
@@ -547,11 +553,11 @@
             pltpu.VMEM((SIDE, SIDE, NB, 128), f32),
             pltpu.VMEM((SIDE * SIDE, NB, 128), f32),
             pieces,
-            pltpu.VMEM((2, SIDE, SIDE, NB + NB // 2, 128), f32),
+            pieces,
             square,
             square,
             pltpu.VMEM((NB, 128), f32),
-            pltpu.VMEM((2 * SIDE, NB // 2, 128), f32),
+            pltpu.VMEM((6 * SIDE, NB // 2, 128), f32),
             pltpu.VMEM((128, 128), f32),
             pltpu.VMEM((NB, 128), f32),
             pltpu.VMEM((NB, 128), f32),

time: 52.2 us -> 49 us (0.939)
  the two profiles are of different devices: /device:TPU:1 before, /device:TPU:11 now
where the time goes in v4:
time: 49 us; the launch traced here: 48.9 us
  Pallas kernels  48.3 us (99%)
  between operations  0.64 us (1%)
    pallas_call x1, Pallas kernels, local(): pl.pallas_call(kernel, out_shape=(jax.ShapeDtypeStruct((rows, cols), f32)...  44.5 us
    pallas_call x1, Pallas kernels, local(): pl.pallas_call(update_kernel, out_shape=(jax.ShapeDtypeStruct((rows, cols...  3.82 us

profile of v4, /device:TPU:11, one launch (start us, length us, event | category | flops | bytes accessed | tf_op | source)
XLA Modules:
  0.0 48.9 jit_solution(15196275037032300883)
XLA Ops:
  0.6 44.5 %shard_map.30 = (f32[512,4096]{1,0:T(8,128)S(1)}, bf16[512,384]{1,0:T(8,128)(2,1)S(1)}, bf16[384,4096]{1,0:T(8,128)(2,1)S(1)}, f32[64,512]{1,0:T(8,128)S(1)}) custom-call(f32[512,4096]{1,0:T(8,128)} %a_hbm.1), custom_call_target="tpu_custom_call" | custom-call | tf_op jit(solution)/shard_map/pallas_call | solution.py:534
  45.1 3.8 %shard_map.31 = (f32[512,4096]{1,0:T(8,128)}, f32[64,512]{1,0:T(8,128)}) custom-call(f32[512,4096]{1,0:T(8,128)S(1)} %get-tuple-element.8.a_ref, bf16[512,384]{1,0:T(8,128)(2,1)S(1)} %get-tuple-element.9.x_ref, bf16[384,4096]{1,0:T(8,128)(2,1)S(1)} %get-tuple-element.10.z_ref, f32[64,512]{1,0:T(8,128)S(1)} %get-tuple-element.11.v_ref), custom_call_target="tpu_custom_call" | custom-call | tf_op jit(solution)/shard_map/pallas_call | solution.py:574

commit v5 on v4

--- a/solution.py
+++ b/solution.py
@@ -406,6 +406,10 @@
         came(rbuf.at[slot], SCATTER + slot)
         total = total + rbuf[slot]
     wbuf[k, y, z] = early + dot(k_t, total)
+    for i, j in AROUND:
+        slot = GATHER_W + 4 * i + j
+        launch(remote(wbuf.at[k, y, z], wbuf.at[k, y, z], slot, slot, dev(wrap(z + i), wrap(y + j), k, x)))
+
     corner = dot(k_p, wbuf[k, y, z], NT)
     mine = 4 * k + x
     cbuf[mine] = jnp.concatenate([corner[: NB // 2], corner[NB // 2 :]], axis=1)
@@ -414,10 +418,6 @@
             slot = CORNER + 2 * d + kk
             launch(remote(cbuf.at[mine], cbuf.at[mine], slot, slot, dev(z, y, wrap_core(k + kk), wrap(x + d))))
     launch(remote(cbuf.at[mine], cbuf.at[mine], CORNER + 1, CORNER + 1, sibling))
-
-    for i, j in AROUND:
-        slot = GATHER_W + 4 * i + j
-        launch(remote(wbuf.at[k, y, z], wbuf.at[k, y, z], slot, slot, dev(wrap(z + i), wrap(y + j), k, x)))
 
     rows_local = pltpu.make_async_copy(wbuf.at[k, y, z], wrow.at[z], load_sem.at[8])
 

time: 49 us -> 48.8 us (level)
  no operation moved by 1% of the time
where the time goes in v5:
time: 48.8 us; the launch traced here: 48.7 us
  Pallas kernels  48.1 us (99%)
  between operations  0.64 us (1%)
    pallas_call x1, Pallas kernels, local(): pl.pallas_call(kernel, out_shape=(jax.ShapeDtypeStruct((rows, cols), f32)...  44.3 us
    pallas_call x1, Pallas kernels, local(): pl.pallas_call(update_kernel, out_shape=(jax.ShapeDtypeStruct((rows, cols...  3.82 us

profile of v5, /device:TPU:11, one launch (start us, length us, event | category | flops | bytes accessed | tf_op | source)
XLA Modules:
  0.0 48.7 jit_solution(9178631770610586597)
XLA Ops:
  0.6 44.3 %shard_map.30 = (f32[512,4096]{1,0:T(8,128)S(1)}, bf16[512,384]{1,0:T(8,128)(2,1)S(1)}, bf16[384,4096]{1,0:T(8,128)(2,1)S(1)}, f32[64,512]{1,0:T(8,128)S(1)}) custom-call(f32[512,4096]{1,0:T(8,128)} %a_hbm.1), custom_call_target="tpu_custom_call" | custom-call | tf_op jit(solution)/shard_map/pallas_call | solution.py:534
  44.9 3.8 %shard_map.31 = (f32[512,4096]{1,0:T(8,128)}, f32[64,512]{1,0:T(8,128)}) custom-call(f32[512,4096]{1,0:T(8,128)S(1)} %get-tuple-element.8.a_ref, bf16[512,384]{1,0:T(8,128)(2,1)S(1)} %get-tuple-element.9.x_ref, bf16[384,4096]{1,0:T(8,128)(2,1)S(1)} %get-tuple-element.10.z_ref, f32[64,512]{1,0:T(8,128)S(1)} %get-tuple-element.11.v_ref), custom_call_target="tpu_custom_call" | custom-call | tf_op jit(solution)/shard_map/pallas_call | solution.py:574

commit v6 on v5

--- a/solution.py
+++ b/solution.py
@@ -497,6 +497,9 @@
         pl.when(diagonal)(rows_local.wait)
         pl.when(off_diagonal)(remote(wrow.at[z], wrow.at[z], OWN_ROWS, OWN_ROWS + z, sibling).wait_recv)
 
+    x_hi, x_lo = split(jnp.transpose(stack([v_t, v_t])))
+    for part, there in ((x_hi, 0), (x_lo, 2 * NB), (x_hi, 4 * NB)):
+        x_out[:, there : there + NB] = part[:, :NB]
     own_came()
     w_t = jnp.concatenate([wrow[q] for q in range(SIDE)], axis=1)
     finish()
@@ -505,8 +508,9 @@
         came(cbuf.at[8 + slot], CORNER_P + slot)
         corner = corner + cbuf[8 + slot]
     w_t = w_t - dot(stack([corner[:, :NB], corner[:, NB:]]), v_t)
-    x_hi, x_lo = split(jnp.transpose(stack([v_t, w_t])))
-    x_out[...] = jnp.concatenate([x_hi, x_lo, x_hi], axis=1)
+    x_hi, x_lo = split(jnp.transpose(stack([w_t, w_t])))
+    for part, there in ((x_hi, NB), (x_lo, 3 * NB), (x_hi, 5 * NB)):
+        x_out[:, there : there + NB] = part[:, NB:]
     finish()
 
 

time: 48.8 us -> 49 us (level)
  no operation moved by 1% of the time
where the time goes in v6:
time: 49 us; the launch traced here: 48.9 us
  Pallas kernels  48.2 us (98%)
  between operations  0.64 us (1%)
    pallas_call x1, Pallas kernels, local(): pl.pallas_call(kernel, out_shape=(jax.ShapeDtypeStruct((rows, cols), f32)...  44.4 us
    pallas_call x1, Pallas kernels, local(): pl.pallas_call(update_kernel, out_shape=(jax.ShapeDtypeStruct((rows, cols...  3.82 us

profile of v6, /device:TPU:11, one launch (start us, length us, event | category | flops | bytes accessed | tf_op | source)
XLA Modules:
  0.0 48.9 jit_solution(16414648785971887868)
XLA Ops:
  0.6 44.4 %shard_map.30 = (f32[512,4096]{1,0:T(8,128)S(1)}, bf16[512,384]{1,0:T(8,128)(2,1)S(1)}, bf16[384,4096]{1,0:T(8,128)(2,1)S(1)}, f32[64,512]{1,0:T(8,128)S(1)}) custom-call(f32[512,4096]{1,0:T(8,128)} %a_hbm.1), custom_call_target="tpu_custom_call" | custom-call | tf_op jit(solution)/shard_map/pallas_call | solution.py:538
  45.0 3.8 %shard_map.31 = (f32[512,4096]{1,0:T(8,128)}, f32[64,512]{1,0:T(8,128)}) custom-call(f32[512,4096]{1,0:T(8,128)S(1)} %get-tuple-element.8.a_ref, bf16[512,384]{1,0:T(8,128)(2,1)S(1)} %get-tuple-element.9.x_ref, bf16[384,4096]{1,0:T(8,128)(2,1)S(1)} %get-tuple-element.10.z_ref, f32[64,512]{1,0:T(8,128)S(1)} %get-tuple-element.11.v_ref), custom_call_target="tpu_custom_call" | custom-call | tf_op jit(solution)/shard_map/pallas_call | solution.py:578
